TPU v7x, 512 devices: a whole 4x4x16 slice. The times are simulated.
512 devices in a mesh: ctx: 32 (over x_lo, z), head: 16 (over x_hi, y, core).
Axes of the slice: x: 4 (x_hi: 2, x_lo: 2; x = x_hi * 2 + x_lo), y: 4, z: 16, core: 2. Of those that a mesh axis runs over, the one named last changes fastest.
Arguments:
- q_latent: bfloat16 [4096, 1536], P('ctx'), may hold values from -6 to 6
- latent_bias: float32 [32, 1536], P('ctx'), may hold values from -3 to 3
- norm_gain: float32 [1536], replicated, may hold values from 0.5 to 1.5
- w_q: bfloat16 [1536, 24576], P('ctx', 'head'), may hold values from -0.15625 to 0.15625
- steer: float32 [32, 24576], P('ctx', 'head'), may hold values from -10 to 10
- kv_latent: bfloat16 [4096, 512], P('ctx'), may hold values from -6 to 6
- key_rope: bfloat16 [4096, 64], P('ctx'), may hold values from -10 to 10
- w_uk: bfloat16 [512, 16384], P(None, 'head'), may hold values from -0.25 to 0.25
- w_uv: bfloat16 [512, 16384], P(None, 'head'), may hold values from -0.25 to 0.25
- d_out: bfloat16 [4096, 16384], P('ctx', 'head'), may hold values from -0.29882812 to 0.29882812
- block_mask: int32 [32, 32], replicated, may hold values from 0 to 1, as said below
Outputs:
- grad_steer: float32 [32, 24576], P('ctx', 'head')
- grad_latent_bias: float32 [32, 1536], P('ctx')
Inputs may be any that keep to these rules, and one draw needn't show every extreme that they name: `block_mask`: query block i always attends key block i; its other entries are 1 at a rate drawn per query block among 1/16, 2/16, 4/16 and 7/16.
All inputs are finite; a program needn't handle non-finite values.
Results may differ from a plain program's by a relative error of at most 0.024.
Values may be sent and summed in bfloat16 or wider, within the bound.
A program may use at most 64 MiB of HBM per device.

v0:
```python
import math

import jax
import jax.numpy as jnp
from jax import lax
from jax.sharding import PartitionSpec as P

KVL = 512
NOPE = 128
ROPE = 64
VD = 128
BLK = 128


epsilon = 1e-06
lowest = -1e30


def contract_last(left, right):
    return lax.dot_general(
        left, right, (((1,), (1,)), ((), ())), preferred_element_type=jnp.float32
    )


def shards(
    q_latent, latent_bias, norm_gain, w_q, steer, kv_latent, key_rope, w_uk, w_uv, d_out, block_mask
):
    queries = q_latent.shape[0]
    nblocks = queries // BLK
    head_count = w_uk.shape[1] // NOPE
    head_width = NOPE + ROPE
    score_scale = head_width ** (-0.5)
    row_count = queries * head_count
    shifted = q_latent.astype(jnp.float32) + jnp.repeat(latent_bias, BLK, axis=0)
    inv_rms = lax.rsqrt(jnp.mean(shifted * shifted, axis=1, keepdims=True) + epsilon)
    normed = shifted * inv_rms
    c_query = (normed * norm_gain).astype(jnp.bfloat16)
    full_wq = lax.all_gather(w_q, "ctx", axis=0, tiled=True)
    projected = jnp.dot(c_query, full_wq, preferred_element_type=jnp.float32)
    query_all = (
        (projected + jnp.repeat(steer, BLK, axis=0))
        .astype(jnp.bfloat16)
        .reshape(queries, head_count, head_width)
    )
    q_rope = query_all[:, :, NOPE:].reshape(row_count, ROPE)
    key_up = w_uk.reshape(KVL, head_count, NOPE)
    value_up = w_uv.reshape(KVL, head_count, VD)
    q_absorbed = (
        jnp.einsum(
            "qhn,khn->qhk", query_all[:, :, :NOPE], key_up, preferred_element_type=jnp.float32
        )
        .astype(jnp.bfloat16)
        .reshape(row_count, KVL)
    )
    g_absorbed = (
        jnp.einsum(
            "qhv,khv->qhk",
            d_out.reshape(queries, head_count, VD),
            value_up,
            preferred_element_type=jnp.float32,
        )
        .astype(jnp.bfloat16)
        .reshape(row_count, KVL)
    )
    my_mask = lax.dynamic_slice_in_dim(block_mask, lax.axis_index("ctx") * nblocks, nblocks, 0)
    start_status = (
        jnp.full((row_count,), lowest, jnp.float32),
        jnp.zeros((row_count,), jnp.float32),
        jnp.zeros((row_count,), jnp.float32),
        jnp.zeros((2 * row_count, KVL), jnp.float32),
        jnp.zeros((2 * row_count, ROPE), jnp.float32),
    )
    lat_portion = lax.all_gather(kv_latent, "ctx", axis=0, tiled=True)
    rope_portion = lax.all_gather(key_rope, "ctx", axis=0, tiled=True)
    key_total = lat_portion.shape[0]
    tile_len = math.gcd(key_total, BLK)
    tile_count = key_total // tile_len

    def visit_tile(status, inputs):
        lat_tile, rope_tile, offset = inputs
        key_block = offset * tile_len // BLK
        column = lax.dynamic_index_in_dim(my_mask, key_block, 1, keepdims=False)

        def update(status):
            peak, total_weight, weighted, lat_acc, rope_acc = status
            live_rows = jnp.repeat(column > 0, head_count * BLK)[:, None]
            scores = (
                contract_last(q_absorbed, lat_tile) + contract_last(q_rope, rope_tile)
            ) * score_scale
            scores = jnp.where(live_rows, scores, lowest)
            new_peak = jnp.maximum(peak, jnp.max(scores, axis=1))
            factor = jnp.exp(peak - new_peak)
            weights = jnp.where(live_rows, jnp.exp(scores - new_peak[:, None]), 0.0)
            dots = contract_last(g_absorbed, lat_tile)
            mixed = weights * dots
            total_weight = total_weight * factor + jnp.sum(weights, axis=1)
            weighted = weighted * factor + jnp.sum(mixed, axis=1)
            stacked = jnp.concatenate([mixed, weights], axis=0).astype(jnp.bfloat16)
            doubled = jnp.concatenate([factor, factor])[:, None]
            lat_acc = lat_acc * doubled + jnp.dot(
                stacked, lat_tile, preferred_element_type=jnp.float32
            )
            rope_acc = rope_acc * doubled + jnp.dot(
                stacked, rope_tile, preferred_element_type=jnp.float32
            )
            return (new_peak, total_weight, weighted, lat_acc, rope_acc)

        def keep_status(status):
            return status

        return (lax.cond(jnp.max(column) > 0, update, keep_status, status), None)

    offsets = jnp.arange(tile_count, dtype=jnp.int32)
    tiles = (
        lat_portion.reshape(tile_count, tile_len, KVL),
        rope_portion.reshape(tile_count, tile_len, ROPE),
        offsets,
    )
    result, unused = lax.scan(visit_tile, start_status, tiles)
    peak, total_weight, weighted, lat_acc, rope_acc = result
    ratio = (weighted / total_weight)[:, None]
    inverse = (score_scale / total_weight)[:, None]
    grad_lat = ((lat_acc[:row_count] - ratio * lat_acc[row_count:]) * inverse).astype(jnp.bfloat16)
    grad_rope = (rope_acc[:row_count] - ratio * rope_acc[row_count:]) * inverse
    grad_nope = jnp.einsum(
        "qhk,khn->qhn",
        grad_lat.reshape(queries, head_count, KVL),
        key_up,
        preferred_element_type=jnp.float32,
    )
    grad_query = jnp.concatenate(
        [grad_nope, grad_rope.reshape(queries, head_count, ROPE)], axis=2
    ).reshape(queries, head_count * head_width)
    grad_steer = jnp.sum(grad_query.reshape(nblocks, BLK, head_count * head_width), axis=1)
    grad_round = grad_query.astype(jnp.bfloat16)
    partial_grad = contract_last(grad_round, full_wq)
    latent_grad = lax.psum(partial_grad.astype(jnp.bfloat16), "head").astype(jnp.float32)
    scaled = latent_grad * norm_gain
    project_mean = jnp.mean(scaled * normed, axis=1, keepdims=True)
    grad_shifted = inv_rms * (scaled - normed * project_mean)
    grad_bias = jnp.sum(grad_shifted.reshape(nblocks, BLK, grad_shifted.shape[1]), axis=1)
    return (grad_steer, grad_bias)


def solution(mesh):
    in_specs = (
        P("ctx", None),
        P("ctx", None),
        P(),
        P("ctx", "head"),
        P("ctx", "head"),
        P("ctx", None),
        P("ctx", None),
        P(None, "head"),
        P(None, "head"),
        P("ctx", "head"),
        P(),
    )
    out_specs = (P("ctx", "head"), P("ctx", None))
    return jax.shard_map(shards, mesh=mesh, in_specs=in_specs, out_specs=out_specs, check_vma=False)
```

profile of v0, /device:TPU:1, one launch (start us, length us, event | category | flops | bytes accessed | tf_op | source)
XLA Modules:
  0.0 747.5 jit_solution(12165556950815326860)
XLA Ops:
  10.2 61.3 %all_gather.11 = bf16[4096,64]{0,1:T(8,128)(2,1)S(1)} all-gather(bf16[128,64]{0,1:T(8,128)(2,1)} %param.21), channel_id=1, replica_groups=mesh['ctx'=32,'head'=16] {'ctx'}, dimensions={0}, use_global_device_ids=true | all-gather | bytes 540672 | tf_op jit(solution)/shard_map/all_gather | solution.py:74
  71.5 1.3 copy.36
  72.8 1.5 copy.46
  75.3 1.5 fusion.25
  76.8 60.9 %all-gather.5.cloned.1.call-done = bf16[1536,1536]{1,0:T(8,128)(2,1)} async-done(((bf16[48,1536]{1,0:T(8,128)(2,1)}), bf16[1536,1536]{1,0:T(8,128)(2,1)}) %all-gather.5.cloned.1.call-update) | async-done | bytes 4718608 | tf_op jit(solution)/shard_map/all_gather | solution.py:38
  137.7 3.2 fusion.23
  141.8 2.4 copy_bitcast_fusion
  144.2 127.4 %all-gather.3.cloned.1.call-done = bf16[4096,512]{1,0:T(8,128)(2,1)} async-done(((bf16[128,512]{1,0:T(8,128)(2,1)}), bf16[4096,512]{1,0:T(8,128)(2,1)}) %all-gather.3.cloned.1.call-update) | async-done | bytes 4194320 | tf_op jit(solution)/shard_map/all_gather | solution.py:73
  272.4 2.5 broadcast_in_dim.47
  275.0 150.2 %while.20 = (s32[]{:T(128)}, f32[1024]{0:T(1024)S(1)}, f32[1024]{0:T(1024)S(1)}, f32[1024]{0:T(1024)S(1)}, f32[2048,512]{1,0:T(8,128)}, /*index=5*/f32[2048,64]{...) while((s32[]{:T(128)}, f32[1024]{0:T(1024)S(1)}, ...), condition=%wide.region_7.8_spmd, body=%wide.region_1.7_spmd.sunk | while | flops 593105920 | bytes 15904864 | solution.py:119
  277.4 11.7 %conditional.2 = ((f32[1024]{0:T(1024)S(1)}, f32[1024]{0:T(1024)S(1)}, f32[1024]{0:T(1024)S(1)}, f32[2048,512]{1,0:T(8,128)}, f32[2048,64]{0,1:T(8,128)})) conditional(s32[]{:T(128)} %bitcast.67, (f32[1024]{0:T(1024)S(1)}, f32[1024]{0:T(1024)S(1)}, f32[1024]{0:T(1024)S(1)}, f32[2048,512]{1,0:T(8,128)}, f32[2048,64]{0,1:T(8,128)}) %tuple.56, ...), branch_computations={%region_2.2_spmd, %region_3.6_spmd} | conditional | flops 593105920 | bytes 15904313 | solution.py:111
  278.1 1.0 fusion.12
  279.1 1.4 fusion.39
  280.5 1.4 fusion.4
  282.0 2.2 convolution_add_fusion
  284.1 5.0 multiply_add_fusion
  296.6 11.7 %conditional.2 = ((f32[1024]{0:T(1024)S(1)}, f32[1024]{0:T(1024)S(1)}, f32[1024]{0:T(1024)S(1)}, f32[2048,512]{1,0:T(8,128)}, f32[2048,64]{0,1:T(8,128)})) conditional(s32[]{:T(128)} %bitcast.67, (f32[1024]{0:T(1024)S(1)}, f32[1024]{0:T(1024)S(1)}, f32[1024]{0:T(1024)S(1)}, f32[2048,512]{1,0:T(8,128)}, f32[2048,64]{0,1:T(8,128)}) %tuple.56, ...), branch_computations={%region_2.2_spmd, %region_3.6_spmd} | conditional | flops 593105920 | bytes 15904313 | solution.py:111
  298.3 1.4 fusion.39
  299.7 1.4 fusion.4
  301.1 2.2 convolution_add_fusion
  303.3 5.0 multiply_add_fusion
  330.8 11.7 %conditional.2 = ((f32[1024]{0:T(1024)S(1)}, f32[1024]{0:T(1024)S(1)}, f32[1024]{0:T(1024)S(1)}, f32[2048,512]{1,0:T(8,128)}, f32[2048,64]{0,1:T(8,128)})) conditional(s32[]{:T(128)} %bitcast.67, (f32[1024]{0:T(1024)S(1)}, f32[1024]{0:T(1024)S(1)}, f32[1024]{0:T(1024)S(1)}, f32[2048,512]{1,0:T(8,128)}, f32[2048,64]{0,1:T(8,128)}) %tuple.56, ...), branch_computations={%region_2.2_spmd, %region_3.6_spmd} | conditional | flops 593105920 | bytes 15904313 | solution.py:111
  331.5 1.0 fusion.12
  332.5 1.4 fusion.39
  333.9 1.4 fusion.4
  335.4 2.2 convolution_add_fusion
  337.5 5.0 multiply_add_fusion
  362.6 11.7 %conditional.2 = ((f32[1024]{0:T(1024)S(1)}, f32[1024]{0:T(1024)S(1)}, f32[1024]{0:T(1024)S(1)}, f32[2048,512]{1,0:T(8,128)}, f32[2048,64]{0,1:T(8,128)})) conditional(s32[]{:T(128)} %bitcast.67, (f32[1024]{0:T(1024)S(1)}, f32[1024]{0:T(1024)S(1)}, f32[1024]{0:T(1024)S(1)}, f32[2048,512]{1,0:T(8,128)}, f32[2048,64]{0,1:T(8,128)}) %tuple.56, ...), branch_computations={%region_2.2_spmd, %region_3.6_spmd} | conditional | flops 593105920 | bytes 15904313 | solution.py:111
  364.2 1.4 fusion.39
  365.6 1.4 fusion.4
  367.1 2.2 convolution_add_fusion
  369.2 5.0 multiply_add_fusion
  376.7 11.7 %conditional.2 = ((f32[1024]{0:T(1024)S(1)}, f32[1024]{0:T(1024)S(1)}, f32[1024]{0:T(1024)S(1)}, f32[2048,512]{1,0:T(8,128)}, f32[2048,64]{0,1:T(8,128)})) conditional(s32[]{:T(128)} %bitcast.67, (f32[1024]{0:T(1024)S(1)}, f32[1024]{0:T(1024)S(1)}, f32[1024]{0:T(1024)S(1)}, f32[2048,512]{1,0:T(8,128)}, f32[2048,64]{0,1:T(8,128)}) %tuple.56, ...), branch_computations={%region_2.2_spmd, %region_3.6_spmd} | conditional | flops 593105920 | bytes 15904313 | solution.py:111
  378.4 1.4 fusion.39
  379.8 1.4 fusion.4
  381.3 2.2 convolution_add_fusion
  383.4 5.0 multiply_add_fusion
  408.4 11.7 %conditional.2 = ((f32[1024]{0:T(1024)S(1)}, f32[1024]{0:T(1024)S(1)}, f32[1024]{0:T(1024)S(1)}, f32[2048,512]{1,0:T(8,128)}, f32[2048,64]{0,1:T(8,128)})) conditional(s32[]{:T(128)} %bitcast.67, (f32[1024]{0:T(1024)S(1)}, f32[1024]{0:T(1024)S(1)}, f32[1024]{0:T(1024)S(1)}, f32[2048,512]{1,0:T(8,128)}, f32[2048,64]{0,1:T(8,128)}) %tuple.56, ...), branch_computations={%region_2.2_spmd, %region_3.6_spmd} | conditional | flops 593105920 | bytes 15904313 | solution.py:111
  410.1 1.4 fusion.39
  411.5 1.4 fusion.4
  413.0 2.2 convolution_add_fusion
  415.1 5.0 multiply_add_fusion
  425.2 2.7 fusion.26
  428.4 1.1 subtract_multiply_fusion
  430.0 4.8 convolution_convert_fusion
  435.8 301.9 %all-reduce.2.cloned.1.call-done = bf16[128,1536]{1,0:T(8,128)(2,1)} async-done(((bf16[128,1536]{1,0:T(8,128)(2,1)}), bf16[128,1536]{1,0:T(8,128)(2,1)}) %all-reduce.2.cloned.1.call-update) | async-done | bytes 393232 | tf_op jit(solution)/shard_map/psum | solution.py:137
  737.8 1.3 multiply_reduce_fusion.1
  739.1 1.3 multiply_reduce_fusion
  (167 shorter events, 52.0 us)
Async XLA Ops:
  7.2 68.1 %copy-start = (bf16[512,1024]{1,0:T(8,128)(2,1)S(1)}, bf16[512,1024]{1,0:T(8,128)(2,1)}, u32[]{:S(2)}) copy-start(bf16[512,1024]{1,0:T(8,128)(2,1)} %param.23) | copy-start | bytes 3145732
  7.2 67.9 %copy-start.3 = (bf16[128,1536]{1,0:T(8,128)(2,1)S(1)}, bf16[128,1536]{1,0:T(8,128)(2,1)}, u32[]{:S(2)}) copy-start(bf16[128,1536]{1,0:T(8,128)(2,1)} %param.15) | copy-start | bytes 1179652
  7.2 68.1 %copy-start.5 = (bf16[128,1024]{1,0:T(8,128)(2,1)S(1)}, bf16[128,1024]{1,0:T(8,128)(2,1)}, u32[]{:S(2)}) copy-start(bf16[128,1024]{1,0:T(8,128)(2,1)} %param.24) | copy-start | bytes 786436
  7.2 130.5 %copy-start.6 = (f32[1536]{0:T(1024)S(1)}, f32[1536]{0:T(1024)}, u32[]{:S(2)}) copy-start(f32[1536]{0:T(1024)} %param.17) | copy-start | bytes 18436
  7.2 130.4 %all-gather.5.cloned.1.call-start = ((), (), s32[]{:S(2)}) async-start(), calls=%async_computation.1 | async-start | bytes 4866048 | tf_op jit(solution)/shard_map/all_gather | solution.py:38
  7.9 263.6 %all-gather.3.cloned.1.call-start = ((), (), s32[]{:S(2)}) async-start(), calls=%async_computation | async-start | bytes 4325376 | tf_op jit(solution)/shard_map/all_gather | solution.py:73
  8.7 729.1 %all-reduce.2.cloned.1.call-start = ((), (), s32[]{:S(2)}) async-start(), calls=%async_computation.2 | async-start | bytes 786432 | tf_op jit(solution)/shard_map/psum | solution.py:137
  74.3 67.0 %copy-start.1 = (bf16[512,1024]{0,1:T(8,128)(2,1)}, bf16[512,1024]{0,1:T(8,128)(2,1)S(1)}, u32[]{:S(2)}) copy-start(bf16[512,1024]{0,1:T(8,128)(2,1)S(1)} %copy.46) | copy-start | bytes 3145732
  425.1 2.7 copy-start.2
  429.7 308.1 %copy-start.4 = (bf16[128,1536]{1,0:T(8,128)(2,1)S(1)}, bf16[128,1536]{1,0:T(8,128)(2,1)}, u32[]{:S(2)}) copy-start(bf16[128,1536]{1,0:T(8,128)(2,1)} %param.15) | copy-start | bytes 1179652
Sparse Core Ops, SparseCore 0:
  10.1 127.4 all-gather.4
  139.7 131.8 all-gather.2
  434.9 302.7 all-reduce.1
where the time goes:
time: 751 us; the launch traced here: 747 us
  waiting for transfers between devices  492 us (66%)
  matrix products  76.3 us (10%)
  blocking collectives  61.3 us (8%)
  loops' own time  45 us (6%)
  local copies, waits for them, and re-layouts  31.1 us (4%)
  other arithmetic  28.1 us (4%)
  between operations  13.9 us (2%)
    psum x1, waiting for transfers between devices, shards(): lax.psum(partial_grad.astype(jnp.bfloat16), 'head').astype(jnp.float32)  302 us
    all_gather x1, waiting for transfers between devices, shards(): lat_portion = lax.all_gather(kv_latent, 'ctx', axis=0, tiled=True)  127 us
    all_gather x1, blocking collectives, shards(): rope_portion = lax.all_gather(key_rope, 'ctx', axis=0, tiled=True)  61.3 us
    all_gather x1, waiting for transfers between devices, shards(): full_wq = lax.all_gather(w_q, 'ctx', axis=0, tiled=True)  60.9 us
    another operation x1, loops' own time, shards(): result, unused = lax.scan(visit_tile, start_status, tiles)  40.3 us
    dot_general x6, matrix products, update(): jnp.dot(stacked, lat_tile, preferred_element_type=jnp.float32)  30.1 us
    dot_general x19, matrix products, contract_last(): lax.dot_general(left, right, (((1,), (1,)), ((), ())), preferred_element_...  27.6 us
    gt x32, other arithmetic, visit_tile(): return (lax.cond(jnp.max(column) > 0, update, keep_status, status), None)  19.6 us
  transfers between devices with their start and end apart: 3, of which 3 were waited for; matrix products, arithmetic and copies ran while one was open for 2% of the time, Pallas kernels for 0%

commit v1 on v0

v1 whole, which is shorter than its diff:
```python
import functools
import math

import jax
import jax.numpy as jnp
from jax import lax
from jax.experimental import pallas as pl
from jax.experimental.pallas import tpu as pltpu
from jax.sharding import PartitionSpec as P

KVL = 512
NOPE = 128
ROPE = 64
BLK = 128
WIDE = 640
HALF = 4
HEADW = NOPE + ROPE
QCOLS = HALF * HEADW
QTWO = QCOLS // 2
DCOLS = HALF * NOPE
EPS = 1e-06
LOWEST = -1e30
NZ = 16
NY = 4
MESH = pl.DeviceIdType.MESH
F32 = jnp.float32
BF16 = jnp.bfloat16
ANY = pl.BlockSpec(memory_space=pl.ANY)
HBM = pl.BlockSpec(memory_space=pltpu.HBM)
VM = pl.BlockSpec(memory_space=pltpu.VMEM)


def last_last(left, right):
    return lax.dot_general(left, right, (((1,), (1,)), ((), ())), preferred_element_type=F32)


def place():
    c = lax.axis_index("ctx")
    k = lax.axis_index("head")
    return c, k, c // NZ, lax.rem(c, NZ)


def gather_kernel(
    w_ref, q_ref, b_ref, s_ref, d_ref, kv_ref, kr_ref,
    W, KV, Xq, Xb, Xs, Xd,
    own, rope,
    w_s, w_r, z_s, z_r, y_s, y_r, f_s, f_r, x_s, x_r, c_s, c_r, m_s, m_r, loc,
):
    c, k, a, z = place()
    x_hi = k // 8
    y = lax.rem(k, 8) // 2
    core = lax.rem(k, 2)
    z_right = (a * NZ + lax.rem(z + 1, NZ), k)
    z_left = (a * NZ + lax.rem(z + NZ - 1, NZ), k)
    z_right2 = (a * NZ + lax.rem(z + 2, NZ), k)
    z_left2 = (a * NZ + lax.rem(z + NZ - 2, NZ), k)
    y_right = (c, x_hi * 8 + lax.rem(y + 1, NY) * 2 + core)
    y_left = (c, x_hi * 8 + lax.rem(y + NY - 1, NY) * 2 + core)
    sibling = (c, x_hi * 8 + y * 2 + (1 - core))
    pair = ((1 - a) * NZ + z, k)
    across = ((1 - a) * NZ + z, (1 - x_hi) * 8 + y * 2 + core)

    barrier = pltpu.get_barrier_semaphore()
    for dev in (z_right, z_left, z_right2, z_left2, y_right, y_left, sibling, pair, across):
        pl.semaphore_signal(barrier, inc=1, device_id=dev, device_id_type=MESH)

    load_k = pltpu.make_async_copy(kv_ref, own.at[:, pl.ds(0, KVL)], loc.at[2])
    load_r = pltpu.make_async_copy(kr_ref, rope, loc.at[3])
    load_k.start()
    load_r.start()
    load_r.wait()
    own[:, KVL:] = jnp.concatenate([rope[...], jnp.zeros((BLK, WIDE - KVL - ROPE), BF16)], axis=1)
    load_k.wait()
    pl.semaphore_wait(barrier, 9)

    sends = []

    def send(src, dst, s, r, dev):
        copy = pltpu.make_async_remote_copy(
            src_ref=src, dst_ref=dst, send_sem=s, recv_sem=r, device_id=dev, device_id_type=MESH
        )
        copy.start()
        sends.append(copy)

    def got(dst, s, r):
        pltpu.make_async_remote_copy(
            src_ref=dst, dst_ref=dst, send_sem=s, recv_sem=r, device_id=pair, device_id_type=MESH
        ).wait_recv()

    def columns(who, two):
        return pl.ds(pl.multiple_of(who * QCOLS + two * QTWO, 128), QTWO)

    their_d = pl.ds(pl.multiple_of((1 - a) * DCOLS, 128), DCOLS)

    counts = {(0, 0): 8, (0, 1): 7, (1, 0): 7, (1, 1): 8}

    def w_slot(part, two, zz):
        return W.at[two, (a if part == 0 else 1 - a) * NZ + lax.rem(zz + 2 * NZ, NZ)]

    def w_send(way, part, two, step):
        at = z - (step - 1) if way == 0 else z + (step - 1)
        slot = w_slot(part, two, at)
        src = w_ref.at[:, columns(a, two)] if step == 1 and part == 0 else slot
        n = 4 * way + 2 * part + two
        send(src, slot, w_s.at[n, step - 1], w_r.at[n, step - 1], z_left if way else z_right)

    def w(step):
        for part, two in ((0, 0), (0, 1), (1, 0), (1, 1)):
            for way in (0, 1):
                if step <= counts[way, part]:
                    n = 4 * way + 2 * part + two
                    at = z + step if way else z - step
                    got(w_slot(part, two, at), w_s.at[n, step - 1], w_r.at[n, step - 1])
                    if step + 1 <= counts[way, part]:
                        w_send(way, part, two, step + 1)

    rows = pl.ds(pl.multiple_of(core * 64 + y * 16, 16), 16)

    def far(way, step):
        return 0 if step == 0 else (2 * step if way else 2 * step - 1)

    def z_send(way, step):
        hop = 1 if step == 1 else 2
        src = own.at[rows] if step <= 2 else KV.at[a, far(way, step - 2), rows]
        dev = (z_left if way else z_right) if hop == 1 else (z_left2 if way else z_right2)
        send(src, KV.at[a, far(way, step), rows], z_s.at[way, step - 1], z_r.at[way, step - 1], dev)

    def kz(step):
        for way in range(2):
            if step <= 8 - way:
                got(KV.at[a, far(way, step), rows], z_s.at[way, step - 1], z_r.at[way, step - 1])
                if step + 2 <= 8 - way:
                    z_send(way, step + 2)

    def y_rows(shift):
        return pl.ds(pl.multiple_of(core * 64 + lax.rem(y + shift + NY, NY) * 16, 16), 16)

    def ky(q):
        part = KV.at[a, pl.ds(4 * q, 4), rows]
        send(part, part, y_s.at[0, q], y_r.at[0, q], y_right)
        send(part, part, y_s.at[1, q], y_r.at[1, q], y_left)

    def kf(q):
        for way in range(2):
            shift = 1 if way else -1
            got(KV.at[a, pl.ds(4 * q, 4), y_rows(shift)], y_s.at[way, q], y_r.at[way, q])
            part = KV.at[a, pl.ds(4 * q + 2 * way, 2), y_rows(shift)]
            send(part, part, f_s.at[way, q], f_r.at[way, q], y_left if way else y_right)

    half = pl.ds(pl.multiple_of(core * 64, 16), 64)

    def split(q):
        near = 16 if q < 2 else 32
        return (
            pl.ds(pl.multiple_of(core * 64, 16), near),
            pl.ds(pl.multiple_of(core * 64 + near, 16), 64 - near),
        )

    def kx(q):
        for way in range(2):
            got(KV.at[a, pl.ds(4 * q + 2 * way, 2), y_rows(2)], f_s.at[way, q], f_r.at[way, q])
        near_rows, far_rows = split(q)
        part = KV.at[a, pl.ds(4 * q, 4), far_rows]
        send(part, part, x_s.at[1, q], x_r.at[1, q], across)
        part = KV.at[a, pl.ds(4 * q, 4), near_rows]
        send(part, part, x_s.at[0, q], x_r.at[0, q], pair)
        part = KV.at[a, pl.ds(4 * q, 4), half]
        send(part, part, c_s.at[0, q], c_r.at[0, q], sibling)

    def kc(q):
        near_rows, far_rows = split(q)
        got(KV.at[1 - a, pl.ds(4 * q, 4), near_rows], x_s.at[0, q], x_r.at[0, q])
        got(KV.at[1 - a, pl.ds(4 * q, 4), far_rows], x_s.at[1, q], x_r.at[1, q])
        part = KV.at[1 - a, pl.ds(4 * q, 4), half]
        send(part, part, c_s.at[1, q], c_r.at[1, q], sibling)

    for two in range(2):
        send(w_ref.at[:, columns(1 - a, two)], W.at[two, c], m_s.at[6 * two], m_r.at[6 * two], pair)
    for step in (1, 2):
        z_send(0, step)
        z_send(1, step)
    for two in range(2):
        w_send(0, 0, two, 1)
        w_send(1, 0, two, 1)
    copy_w = [pltpu.make_async_copy(w_ref.at[:, columns(a, two)], W.at[two, c], loc.at[4 * two]) for two in range(2)]
    for copy in copy_w:
        copy.start()
    copy_k = pltpu.make_async_copy(own.at[rows], KV.at[a, 0, rows], loc.at[1])
    copy_k.start()
    q_rows = pl.ds(pl.multiple_of(core * 64, 16), 64)
    send(q_ref.at[q_rows], Xq.at[q_rows], m_s.at[1], m_r.at[1], pair)
    send(d_ref.at[:, their_d], Xd, m_s.at[3], m_r.at[3], pair)
    send(b_ref, Xb, m_s.at[4], m_r.at[4], pair)
    send(s_ref, Xs, m_s.at[5], m_r.at[5], pair)
    for two in range(2):
        got(w_slot(1, two, z), m_s.at[6 * two], m_r.at[6 * two])
        w_send(0, 1, two, 1)
        w_send(1, 1, two, 1)

    kz(1)
    w(1)
    kz(2)
    copy_k.wait()
    ky(0)
    w(2)
    kz(3)
    kf(0)
    kz(4)
    ky(1)
    w(3)
    kx(0)
    kz(5)
    kf(1)
    kz(6)
    ky(2)
    w(4)
    kx(1)
    kc(0)
    kz(7)
    kf(2)
    kz(8)
    ky(3)
    w(5)
    kc(1)
    got(Xq.at[q_rows], m_s.at[1], m_r.at[1])
    send(Xq.at[q_rows], Xq.at[q_rows], m_s.at[2], m_r.at[2], sibling)
    kx(2)
    w(6)
    kf(3)
    kc(2)
    w(7)
    kx(3)
    w(8)
    kc(3)

    other = pl.ds(pl.multiple_of((1 - core) * 64, 16), 64)
    for q in range(4):
        got(KV.at[a, pl.ds(4 * q, 4), other], c_s.at[0, q], c_r.at[0, q])
        got(KV.at[1 - a, pl.ds(4 * q, 4), other], c_s.at[1, q], c_r.at[1, q])
    got(Xq.at[other], m_s.at[2], m_r.at[2])
    got(Xd, m_s.at[3], m_r.at[3])
    got(Xb, m_s.at[4], m_r.at[4])
    got(Xs, m_s.at[5], m_r.at[5])
    for copy in copy_w:
        copy.wait()
    for copy in sends:
        copy.wait_send()


def gather(w_q, q_latent, latent_bias, steer, d_out, kv_latent, key_rope):
    def dma(*shape):
        return pltpu.SemaphoreType.DMA(shape)

    return pl.pallas_call(
        gather_kernel,
        out_shape=(
            jax.ShapeDtypeStruct((2, 2 * NZ, w_q.shape[0], QTWO), BF16),
            jax.ShapeDtypeStruct((2, NZ, BLK, WIDE), BF16),
            jax.ShapeDtypeStruct(q_latent.shape, BF16),
            jax.ShapeDtypeStruct(latent_bias.shape, F32),
            jax.ShapeDtypeStruct(steer.shape, F32),
            jax.ShapeDtypeStruct((BLK, DCOLS), BF16),
        ),
        in_specs=[HBM] * 7,
        out_specs=[ANY] * 6,
        scratch_shapes=[
            pltpu.VMEM((BLK, WIDE), BF16),
            pltpu.VMEM((BLK, ROPE), BF16),
            dma(8, 8), dma(8, 8), dma(2, 8), dma(2, 8), dma(2, 4), dma(2, 4), dma(2, 4), dma(2, 4),
            dma(2, 4), dma(2, 4), dma(2, 4), dma(2, 4), dma(7), dma(7), dma(5),
        ],
        compiler_params=pltpu.CompilerParams(
            collective_id=0, has_side_effects=True, vmem_limit_bytes=54 * 2**20
        ),
        cost_estimate=pl.CostEstimate(flops=0, bytes_accessed=20_000_000, transcendentals=0),
        name="gather",
    )(w_q, q_latent, latent_bias, steer, d_out, kv_latent, key_rope)


CHUNK = 256
TILES = CHUNK // BLK


def attend_kernel(
    mask, q_ref, xq_ref, b_ref, xb_ref, gain_ref, W_ref, s_ref, xs_ref, KV, uk_ref, uv_ref, d_ref, xd_ref,
    gs_ref, lb_ref,
    Wv, q2, uk, uv, dv, kvc, cq, pj, qg, qr, sbuf, dbuf, acc, gl, gr, peak, lsum, gsum, u_ref,
    sem, kv_sem,
):
    c, k, a, z = place()
    gain = gain_ref[...].reshape(1, gain_ref.shape[0])
    scale = HEADW ** (-0.5)
    scale2 = scale * math.log2(math.e)
    rows = HALF * BLK
    my_d = pl.ds(pl.multiple_of(a * DCOLS, 128), DCOLS)
    loads = [
        pltpu.make_async_copy(q_ref, q2.at[0], sem.at[0]),
        pltpu.make_async_copy(W_ref, Wv, sem.at[1]),
        pltpu.make_async_copy(uk_ref.at[:, my_d], uk, sem.at[2]),
        pltpu.make_async_copy(uv_ref.at[:, my_d], uv, sem.at[3]),
        pltpu.make_async_copy(d_ref.at[:, my_d], dv.at[0], sem.at[4]),
        pltpu.make_async_copy(xq_ref, q2.at[1], sem.at[5]),
        pltpu.make_async_copy(xd_ref, dv.at[1], sem.at[6]),
    ]
    for copy in loads:
        copy.start()

    def tile_copy(i, j, n):
        far = lax.rem(z - lax.rem(j, NZ) + NZ, NZ)
        slot = jnp.where(far == 0, 0, jnp.where(far <= NZ // 2, 2 * far - 1, 2 * (NZ - far)))
        return pltpu.make_async_copy(KV.at[j // NZ, slot], kvc.at[i, n], kv_sem.at[i, n])

    live = []
    for i in range(2):
        block = c if i == 0 else lax.rem(c + NZ, 2 * NZ)

        def visit(j, n):
            on = mask[block, j] > 0

            @pl.when(on)
            def _():
                tile_copy(i, j, n).start()

            return n + jnp.where(on, 1, 0)

        live.append(lax.fori_loop(0, 2 * NZ, visit, 0))

    def chunks_of(n):
        return (n + TILES - 1) // TILES

    for i in range(2):
        n = live[i]
        for extra in range(TILES - 1):
            @pl.when(n + extra < chunks_of(n) * TILES)
            def _():
                kvc[i, n + extra] = jnp.zeros((BLK, WIDE), BF16)

    def keys_of(i, t):
        return kvc[i, pl.ds(t * TILES, TILES)].reshape(CHUNK, WIDE)

    invs = []
    for i in range(2):
        loads[5 * i].wait()
        shifted = q2[i].astype(F32) + (b_ref, xb_ref)[i][...]
        invs.append(lax.rsqrt(jnp.mean(shifted * shifted, axis=1, keepdims=True) + EPS))
        cq[i] = (shifted * invs[i] * gain).astype(BF16)
    both = 2 * BLK
    loads[3].wait()
    loads[4].wait()
    loads[6].wait()
    for h in range(HALF):
        up = slice(h * NOPE, (h + 1) * NOPE)
        g = last_last(dv[:, :, up].reshape(both, NOPE), uv[:, up]).astype(BF16)
        for i in range(2):
            qg[i, rows + h * BLK : rows + (h + 1) * BLK, :] = g[i * BLK : (i + 1) * BLK]
    loads[1].wait()
    loads[2].wait()
    c_query = cq[...].reshape(both, cq.shape[2])
    for two in range(2):
        proj = jnp.dot(c_query, Wv[two], preferred_element_type=F32)
        pj[:, two * QTWO : (two + 1) * QTWO] = proj
        for i in range(2):
            row = (s_ref, xs_ref)[i]
            part = slice(two * QTWO, (two + 1) * QTWO)
            other = slice(QCOLS + two * QTWO, QCOLS + (two + 1) * QTWO)
            cq[i, :, part] = (proj[i * BLK : (i + 1) * BLK] + jnp.where(a == 0, row[:, part], row[:, other])).astype(BF16)
    query = cq[:, :, :QCOLS].reshape(both, QCOLS)
    for h in range(HALF):
        at = h * HEADW
        q = last_last(query[:, at : at + NOPE], uk[:, h * NOPE : (h + 1) * NOPE]).astype(BF16)
        rope = query[:, at + NOPE : at + HEADW]
        rope = jnp.concatenate([rope, jnp.zeros((both, WIDE - KVL - ROPE), BF16)], axis=1)
        for i in range(2):
            qg[i, h * BLK : (h + 1) * BLK, :] = q[i * BLK : (i + 1) * BLK]
            qr[i, h * BLK : (h + 1) * BLK, :] = rope[i * BLK : (i + 1) * BLK]

    def in_pairs(count, step):
        def pair(t, _):
            step(2 * t, 2)
            return 0

        lax.fori_loop(0, count // 2, pair, 0)

        @pl.when(lax.rem(count, 2) == 1)
        def _():
            step(count - 1, 1)

    for i in range(2):
        n = live[i]
        count = chunks_of(n)

        def arrived(t, _):
            tile_copy(i, 0, t).wait()
            return 0

        lax.fori_loop(0, n, arrived, 0)
        peak[...] = jnp.full((rows, 128), LOWEST, F32)
        lsum[...] = jnp.zeros((rows, 128), F32)
        gsum[...] = jnp.zeros((rows, 128), F32)
        acc[...] = jnp.zeros((rows, WIDE), F32)

        def scores(first, many):
            top = peak[...]
            for t in [first + d for d in range(many)]:
                keys = keys_of(i, t)
                column = lax.broadcasted_iota(jnp.int32, (1, CHUNK), 1) + t * CHUNK
                dead = jnp.where(column < n * BLK, 0.0, LOWEST)
                main = last_last(qg[i], keys[:, :KVL])
                s = main[:rows] + last_last(qr[i], keys[:, KVL:]) + dead
                sbuf[t] = s
                dbuf[t] = main[rows:]
                for part in range(TILES):
                    top = jnp.maximum(top, s[:, part * 128 : (part + 1) * 128])
            peak[...] = top

        in_pairs(count, scores)
        top = jnp.max(peak[...], axis=1, keepdims=True) * scale2

        def weigh(first, many):
            low = lsum[...]
            gow = gsum[...]
            for t in [first + d for d in range(many)]:
                e = jnp.exp2(sbuf[t] * scale2 - top)
                sbuf[t] = e
                mixed = e * dbuf[t]
                low = low + sum(e[:, p * 128 : (p + 1) * 128] for p in range(TILES))
                gow = gow + sum(mixed[:, p * 128 : (p + 1) * 128] for p in range(TILES))
            lsum[...] = low
            gsum[...] = gow

        in_pairs(count, weigh)
        total = jnp.sum(lsum[...], axis=1, keepdims=True)
        ratio = jnp.sum(gsum[...], axis=1, keepdims=True) / total

        def collect(first, many):
            weight = jnp.concatenate(
                [(sbuf[first + d] * (dbuf[first + d] - ratio)).astype(BF16) for d in range(many)], axis=1
            )
            keys = kvc[i, pl.ds(first * TILES, many * TILES)].reshape(many * CHUNK, WIDE)
            acc[...] += jnp.dot(weight, keys, preferred_element_type=F32)

        in_pairs(count, collect)
        grad = acc[...] * (scale / total)
        gl[i] = grad[:, :KVL].astype(BF16).reshape(HALF, BLK, KVL)
        gr[i] = grad[:, KVL:].reshape(HALF, BLK, WIDE - KVL)

    pieces = []
    for h in range(HALF):
        pieces.append(
            jnp.dot(gl[:, h].reshape(both, KVL), uk[:, h * NOPE : (h + 1) * NOPE], preferred_element_type=F32)
        )
        pieces.append(gr[:, h].reshape(both, WIDE - KVL)[:, :ROPE])
    all_grads = jnp.concatenate(pieces, axis=1)
    for i in range(2):
        grad_query = all_grads[i * BLK : (i + 1) * BLK]
        gs_ref[i : i + 1, :] = jnp.sum(grad_query, axis=0, keepdims=True)
        lean = jnp.sum(grad_query * pj[i * BLK : (i + 1) * BLK, :], axis=1, keepdims=True)
        u = jnp.sum(grad_query * invs[i], axis=0, keepdims=True)
        u_high = u.astype(BF16)
        u_ref[2 * i : 2 * i + 1, :] = u_high.astype(F32)
        u_ref[2 * i + 1 : 2 * i + 2, :] = u - u_high.astype(F32)
        shifted = q2[i].astype(F32) + (b_ref, xb_ref)[i][...]
        lb_ref[i : i + 1, :] = jnp.sum(shifted * (invs[i] * invs[i] * lean), axis=0, keepdims=True)

    back = sum(
        last_last(u_ref[:, two * QTWO : (two + 1) * QTWO].astype(BF16), Wv[two]) for two in range(2)
    )
    for i in range(2):
        whole = back[2 * i : 2 * i + 1] + back[2 * i + 1 : 2 * i + 2]
        lb_ref[i : i + 1, :] = gain * whole - lb_ref[i : i + 1, :] * (1.0 / gain.shape[1])


def attend(mask, q, xq, b, xb, gain, W, s, xs, KV, w_uk, w_uv, d, xd):
    ql = q.shape[1]
    rows = HALF * BLK
    nchunk = 2 * NZ // TILES
    return pl.pallas_call(
        attend_kernel,
        out_shape=(jax.ShapeDtypeStruct((2, QCOLS), F32), jax.ShapeDtypeStruct((2, ql), F32)),
        in_specs=[
            pl.BlockSpec(memory_space=pltpu.SMEM), HBM, ANY, VM, VM, VM, ANY, VM, VM, ANY, HBM, HBM, HBM, ANY,
        ],
        out_specs=[VM, VM],
        scratch_shapes=[
            pltpu.VMEM((2, ql, QTWO), BF16),
            pltpu.VMEM((2, BLK, ql), BF16),
            pltpu.VMEM((KVL, DCOLS), BF16),
            pltpu.VMEM((KVL, DCOLS), BF16),
            pltpu.VMEM((2, BLK, DCOLS), BF16),
            pltpu.VMEM((2, 2 * NZ, BLK, WIDE), BF16),
            pltpu.VMEM((2, BLK, ql), BF16),
            pltpu.VMEM((2 * BLK, QCOLS), F32),
            pltpu.VMEM((2, 2 * rows, KVL), BF16),
            pltpu.VMEM((2, rows, WIDE - KVL), BF16),
            pltpu.VMEM((nchunk, rows, CHUNK), F32),
            pltpu.VMEM((nchunk, rows, CHUNK), F32),
            pltpu.VMEM((rows, WIDE), F32),
            pltpu.VMEM((2, HALF, BLK, KVL), BF16),
            pltpu.VMEM((2, HALF, BLK, WIDE - KVL), F32),
            pltpu.VMEM((rows, 128), F32),
            pltpu.VMEM((rows, 128), F32),
            pltpu.VMEM((rows, 128), F32),
            pltpu.VMEM((16, QCOLS), F32),
            pltpu.SemaphoreType.DMA((7,)),
            pltpu.SemaphoreType.DMA((2, 2 * NZ)),
        ],
        compiler_params=pltpu.CompilerParams(vmem_limit_bytes=54 * 2**20),
        cost_estimate=pl.CostEstimate(flops=10_000_000_000, bytes_accessed=10_000_000, transcendentals=4_000_000),
        name="attend",
    )(mask, q, xq, b, xb, gain, W, s, xs, KV, w_uk, w_uv, d, xd)


def reduce_kernel(gs_ref, lb_ref, steer_out, bias_out, total, rbuf, rgs, rlb, p_s, p_r, g_s, g_r):
    c, k, a, z = place()
    pair = ((1 - a) * NZ + z, k)
    n = 16

    def mate(shift):
        return (c, lax.rem(k + shift + n, n))

    barrier = pltpu.get_barrier_semaphore()
    pl.semaphore_signal(barrier, inc=1, device_id=pair, device_id_type=MESH)
    for shift in range(1, n):
        pl.semaphore_signal(barrier, inc=1, device_id=mate(shift), device_id_type=MESH)
    pl.semaphore_wait(barrier, n)

    def copy(src, dst, s, r, dev):
        return pltpu.make_async_remote_copy(
            src_ref=src, dst_ref=dst, send_sem=s, recv_sem=r, device_id=dev, device_id_type=MESH
        )

    first = copy(lb_ref.at[pl.ds(1, 1)], rlb, p_s.at[0], p_r.at[0], pair)
    second = copy(gs_ref.at[pl.ds(1, 1)], rgs, p_s.at[1], p_r.at[1], pair)
    first.start()
    second.start()
    first.wait_recv()
    total[...] = lb_ref[0:1, :] + rlb[...]
    out = []
    for shift in range(1, n):
        out.append(copy(total, rbuf.at[shift], g_s.at[shift], g_r.at[shift], mate(shift)))
        out[-1].start()
    second.wait_recv()
    mine = gs_ref[0:1, :]
    theirs = rgs[...]
    steer_out[:, :QCOLS] = jnp.where(a == 0, mine, theirs)
    steer_out[:, QCOLS:] = jnp.where(a == 0, theirs, mine)
    result = total[...]
    for shift in range(1, n):
        out[shift - 1].wait_recv()
        result = result + rbuf[shift]
    bias_out[...] = result
    first.wait_send()
    second.wait_send()
    for one in out:
        one.wait_send()


def reduce(gs, lb):
    ql = lb.shape[1]
    return pl.pallas_call(
        reduce_kernel,
        out_shape=(jax.ShapeDtypeStruct((1, 2 * QCOLS), F32), jax.ShapeDtypeStruct((1, ql), F32)),
        in_specs=[VM, VM],
        out_specs=[VM, VM],
        scratch_shapes=[
            pltpu.VMEM((1, ql), F32),
            pltpu.VMEM((16, 1, ql), F32),
            pltpu.VMEM((1, QCOLS), F32),
            pltpu.VMEM((1, ql), F32),
            pltpu.SemaphoreType.DMA((2,)),
            pltpu.SemaphoreType.DMA((2,)),
            pltpu.SemaphoreType.DMA((16,)),
            pltpu.SemaphoreType.DMA((16,)),
        ],
        compiler_params=pltpu.CompilerParams(collective_id=1, has_side_effects=True),
        name="reduce",
    )(gs, lb)


def shards(
    q_latent, latent_bias, norm_gain, w_q, steer, kv_latent, key_rope, w_uk, w_uv, d_out, block_mask
):
    ql = q_latent.shape[1]
    W, KV, Xq, Xb, Xs, Xd = gather(w_q, q_latent, latent_bias, steer, d_out, kv_latent, key_rope)
    gs, lb = attend(
        block_mask, q_latent, Xq, latent_bias, Xb, norm_gain, W.reshape(2, ql, QTWO), steer, Xs,
        KV, w_uk, w_uv, d_out, Xd,
    )
    grad_steer, grad_bias = reduce(gs, lb)
    return (grad_steer, grad_bias)


def solution(mesh):
    in_specs = (
        P("ctx", None),
        P("ctx", None),
        P(),
        P("ctx", "head"),
        P("ctx", "head"),
        P("ctx", None),
        P("ctx", None),
        P(None, "head"),
        P(None, "head"),
        P("ctx", "head"),
        P(),
    )
    out_specs = (P("ctx", "head"), P("ctx", None))
    return jax.shard_map(shards, mesh=mesh, in_specs=in_specs, out_specs=out_specs, check_vma=False)
```

time: 751 us -> 96.6 us (0.13)
  the two profiles are of different devices: /device:TPU:1 before, /device:TPU:35 now
where the time goes in v1:
time: 96.6 us; the launch traced here: 96.1 us
  Pallas kernels  91.5 us (95%)
  local copies, waits for them, and re-layouts  4 us (4%)
    pallas_call x1, Pallas kernels, gather(): pl.pallas_call(gather_kernel, out_shape=(jax.ShapeDtypeStruct((2, 2 * NZ,...  56 us
    pallas_call x1, Pallas kernels, attend(): pl.pallas_call(attend_kernel, out_shape=(jax.ShapeDtypeStruct((2, QCOLS),...  21.9 us
    pallas_call x1, Pallas kernels, reduce(): pl.pallas_call(reduce_kernel, out_shape=(jax.ShapeDtypeStruct((1, 2 * QCO...  13.6 us
    unnamed x3, local copies, waits for them, and re-layouts  4 us

profile of v1, /device:TPU:35, one launch (start us, length us, event | category | flops | bytes accessed | tf_op | source)
XLA Modules:
  0.0 96.1 jit_solution(9052856319318742910)
XLA Ops:
  0.6 1.4 %copy.13.kr_ref = bf16[128,64]{1,0:T(8,128)(2,1)} copy(bf16[128,64]{0,1:T(8,128)(2,1)} %param.17) | data formatting | bytes 32768 | tf_op args[6]
  2.1 56.0 %gather.1 = (bf16[2,32,48,384]{3,2,1,0:T(8,128)(2,1)}, bf16[2,16,128,640]{3,2,1,0:T(8,128)(2,1)}, bf16[128,1536]{1,0:T(8,128)(2,1)}, f32[1,1536]{1,0:T(1,128)}, ...) custom-call(bf16[48,1536]{1,0:T(8,128)(2,1)} %w_ref.1, bf16[128,1536]{1,0:T(8,128)(2,1)} %q_ref.3, f32[1,1536]{1,0:T(1,128)} %b_ref.3, ...), custom_call_target="tpu_custom_call" | custom-call | bytes 20000000 | tf_op jit(solution)/shard_map/gather/pallas_call | solution.py:254
  58.1 21.9 %attend.1 = (f32[2,768]{1,0:T(2,128)}, f32[2,1536]{1,0:T(2,128)}) custom-call(s32[32,32]{1,0:T(8,128)} %mask.1, bf16[128,1536]{1,0:T(8,128)(2,1)} %q_ref.3, bf16[128,1536]{1,0:T(8,128)(2,1)} %get-tuple-element.10.xq_ref, f32[1,1536]{1,0:T(1,128)} %b_ref.3, f32[1,1536]{1,0:T(1,128)} %get-tuple-element.11.xb_ref, f32[1536]{0:T(1024)} %gain_ref.1, ...), custom_call_target="tpu_custom_call" | custom-call | flops 10000000000 | bytes 10000000 | tf_op jit(solution)/shard_map/attend/pallas_call | solution.py:477
  79.9 13.6 %reduce.1 = (f32[1,1536]{1,0:T(1,128)}, f32[1,1536]{1,0:T(1,128)}) custom-call(f32[2,768]{1,0:T(2,128)} %get-tuple-element.16.gs_ref, f32[2,1536]{1,0:T(2,128)} %get-tuple-element.17.lb_ref), custom_call_target="tpu_custom_call" | custom-call | tf_op jit(solution)/shard_map/reduce/pallas_call | solution.py:560
  93.6 1.3 %copy.16 = f32[1,1536]{1,0:T(1,128)} copy(f32[1,1536]{1,0:T(1,128)} %get-tuple-element.20) | data formatting | bytes 12288
  94.8 1.3 %copy.17 = f32[1,1536]{1,0:T(1,128)} copy(f32[1,1536]{1,0:T(1,128)} %get-tuple-element.21) | data formatting | bytes 12288

commit v2 on v1

--- a/solution.py
+++ b/solution.py
@@ -69,7 +69,8 @@
     load_k.start()
     load_r.start()
     load_r.wait()
-    own[:, KVL:] = jnp.concatenate([rope[...], jnp.zeros((BLK, WIDE - KVL - ROPE), BF16)], axis=1)
+    tall = jnp.concatenate([rope[...].astype(F32), jnp.zeros((WIDE - KVL - ROPE, BLK), F32)], axis=0)
+    own[:, KVL:] = tall.T.astype(BF16)
     load_k.wait()
     pl.semaphore_wait(barrier, 9)
 
@@ -135,44 +136,40 @@
     def y_rows(shift):
         return pl.ds(pl.multiple_of(core * 64 + lax.rem(y + shift + NY, NY) * 16, 16), 16)
 
-    def ky(q):
-        part = KV.at[a, pl.ds(4 * q, 4), rows]
-        send(part, part, y_s.at[0, q], y_r.at[0, q], y_right)
-        send(part, part, y_s.at[1, q], y_r.at[1, q], y_left)
-
-    def kf(q):
+    def block(far_side, first, count, row):
+        return KV.at[1 - a if far_side else a, pl.ds(first, count), row]
+
+    def kx(q):
+        for n, dev in ((0, pair), (1, across)):
+            part = block(0, 4 * q + 2 * n, 2, rows)
+            send(part, part, x_s.at[n, q], x_r.at[n, q], dev)
+
+    def ky(q, far_side):
+        if far_side:
+            for n in range(2):
+                got(block(1, 4 * q + 2 * n, 2, rows), x_s.at[n, q], x_r.at[n, q])
+        part = block(far_side, 4 * q, 4, rows)
         for way in range(2):
-            shift = 1 if way else -1
-            got(KV.at[a, pl.ds(4 * q, 4), y_rows(shift)], y_s.at[way, q], y_r.at[way, q])
-            part = KV.at[a, pl.ds(4 * q + 2 * way, 2), y_rows(shift)]
-            send(part, part, f_s.at[way, q], f_r.at[way, q], y_left if way else y_right)
+            n = 2 * far_side + way
+            send(part, part, y_s.at[n, q], y_r.at[n, q], y_left if way else y_right)
+
+    def kf(q, far_side):
+        for way in range(2):
+            n = 2 * far_side + way
+            row = y_rows(1 if way else -1)
+            got(block(far_side, 4 * q, 4, row), y_s.at[n, q], y_r.at[n, q])
+            part = block(far_side, 4 * q + 2 * way, 2, row)
+            send(part, part, f_s.at[n, q], f_r.at[n, q], y_left if way else y_right)
 
     half = pl.ds(pl.multiple_of(core * 64, 16), 64)
 
-    def split(q):
-        near = 16 if q < 2 else 32
-        return (
-            pl.ds(pl.multiple_of(core * 64, 16), near),
-            pl.ds(pl.multiple_of(core * 64 + near, 16), 64 - near),
-        )
-
-    def kx(q):
-        for way in range(2):
-            got(KV.at[a, pl.ds(4 * q + 2 * way, 2), y_rows(2)], f_s.at[way, q], f_r.at[way, q])
-        near_rows, far_rows = split(q)
-        part = KV.at[a, pl.ds(4 * q, 4), far_rows]
-        send(part, part, x_s.at[1, q], x_r.at[1, q], across)
-        part = KV.at[a, pl.ds(4 * q, 4), near_rows]
-        send(part, part, x_s.at[0, q], x_r.at[0, q], pair)
-        part = KV.at[a, pl.ds(4 * q, 4), half]
-        send(part, part, c_s.at[0, q], c_r.at[0, q], sibling)
-
     def kc(q):
-        near_rows, far_rows = split(q)
-        got(KV.at[1 - a, pl.ds(4 * q, 4), near_rows], x_s.at[0, q], x_r.at[0, q])
-        got(KV.at[1 - a, pl.ds(4 * q, 4), far_rows], x_s.at[1, q], x_r.at[1, q])
-        part = KV.at[1 - a, pl.ds(4 * q, 4), half]
-        send(part, part, c_s.at[1, q], c_r.at[1, q], sibling)
+        for far_side in range(2):
+            for way in range(2):
+                n = 2 * far_side + way
+                got(block(far_side, 4 * q + 2 * way, 2, y_rows(2)), f_s.at[n, q], f_r.at[n, q])
+        part = KV.at[:, pl.ds(4 * q, 4), half]
+        send(part, part, c_s.at[q], c_r.at[q], sibling)
 
     for two in range(2):
         send(w_ref.at[:, columns(1 - a, two)], W.at[two, c], m_s.at[6 * two], m_r.at[6 * two], pair)
@@ -198,45 +195,52 @@
         w_send(1, 1, two, 1)
 
     kz(1)
-    w(1)
     kz(2)
     copy_k.wait()
-    ky(0)
+    kx(0)
+    ky(0, 0)
+    w(1)
+    kz(3)
+    ky(0, 1)
+    kz(4)
+    kx(1)
+    ky(1, 0)
+    kf(0, 0)
     w(2)
-    kz(3)
-    kf(0)
-    kz(4)
-    ky(1)
+    kz(5)
+    ky(1, 1)
+    kz(6)
+    kx(2)
+    ky(2, 0)
+    kf(0, 1)
+    kf(1, 0)
     w(3)
-    kx(0)
-    kz(5)
-    kf(1)
-    kz(6)
-    ky(2)
+    kz(7)
+    ky(2, 1)
+    kz(8)
+    kx(3)
+    ky(3, 0)
+    kf(1, 1)
+    kf(2, 0)
     w(4)
-    kx(1)
     kc(0)
-    kz(7)
-    kf(2)
-    kz(8)
-    ky(3)
+    ky(3, 1)
+    got(Xq.at[q_rows], m_s.at[1], m_r.at[1])
+    send(Xq.at[q_rows], Xq.at[q_rows], m_s.at[2], m_r.at[2], sibling)
+    kf(2, 1)
+    kf(3, 0)
     w(5)
     kc(1)
-    got(Xq.at[q_rows], m_s.at[1], m_r.at[1])
-    send(Xq.at[q_rows], Xq.at[q_rows], m_s.at[2], m_r.at[2], sibling)
-    kx(2)
     w(6)
-    kf(3)
+    kf(3, 1)
     kc(2)
     w(7)
-    kx(3)
+    kc(3)
     w(8)
-    kc(3)
 
     other = pl.ds(pl.multiple_of((1 - core) * 64, 16), 64)
     for q in range(4):
-        got(KV.at[a, pl.ds(4 * q, 4), other], c_s.at[0, q], c_r.at[0, q])
-        got(KV.at[1 - a, pl.ds(4 * q, 4), other], c_s.at[1, q], c_r.at[1, q])
+        got(KV.at[:, pl.ds(4 * q, 4), other], c_s.at[q], c_r.at[q])
     got(Xq.at[other], m_s.at[2], m_r.at[2])
     got(Xd, m_s.at[3], m_r.at[3])
     got(Xb, m_s.at[4], m_r.at[4])
@@ -265,9 +269,9 @@
         out_specs=[ANY] * 6,
         scratch_shapes=[
             pltpu.VMEM((BLK, WIDE), BF16),
-            pltpu.VMEM((BLK, ROPE), BF16),
-            dma(8, 8), dma(8, 8), dma(2, 8), dma(2, 8), dma(2, 4), dma(2, 4), dma(2, 4), dma(2, 4),
-            dma(2, 4), dma(2, 4), dma(2, 4), dma(2, 4), dma(7), dma(7), dma(5),
+            pltpu.VMEM((ROPE, BLK), BF16),
+            dma(8, 8), dma(8, 8), dma(2, 8), dma(2, 8), dma(4, 4), dma(4, 4), dma(4, 4), dma(4, 4),
+            dma(2, 4), dma(2, 4), dma(4), dma(4), dma(7), dma(7), dma(5),
         ],
         compiler_params=pltpu.CompilerParams(
             collective_id=0, has_side_effects=True, vmem_limit_bytes=54 * 2**20
@@ -284,8 +288,8 @@
 def attend_kernel(
     mask, q_ref, xq_ref, b_ref, xb_ref, gain_ref, W_ref, s_ref, xs_ref, KV, uk_ref, uv_ref, d_ref, xd_ref,
     gs_ref, lb_ref,
-    Wv, q2, uk, uv, dv, kvc, cq, pj, qg, qr, sbuf, dbuf, acc, gl, gr, peak, lsum, gsum, u_ref,
-    sem, kv_sem,
+    Wv, q2, uk, uv, dv, keys_all, cq, pj, qg, qr, sbuf, dbuf, acc, gl, gr, peak, lsum, gsum, u_ref,
+    index, sem,
 ):
     c, k, a, z = place()
     gain = gain_ref[...].reshape(1, gain_ref.shape[0])
@@ -301,42 +305,31 @@
         pltpu.make_async_copy(d_ref.at[:, my_d], dv.at[0], sem.at[4]),
         pltpu.make_async_copy(xq_ref, q2.at[1], sem.at[5]),
         pltpu.make_async_copy(xd_ref, dv.at[1], sem.at[6]),
+        pltpu.make_async_copy(KV, keys_all, sem.at[7]),
     ]
     for copy in loads:
         copy.start()
 
-    def tile_copy(i, j, n):
-        far = lax.rem(z - lax.rem(j, NZ) + NZ, NZ)
-        slot = jnp.where(far == 0, 0, jnp.where(far <= NZ // 2, 2 * far - 1, 2 * (NZ - far)))
-        return pltpu.make_async_copy(KV.at[j // NZ, slot], kvc.at[i, n], kv_sem.at[i, n])
-
     live = []
     for i in range(2):
         block = c if i == 0 else lax.rem(c + NZ, 2 * NZ)
 
         def visit(j, n):
-            on = mask[block, j] > 0
-
-            @pl.when(on)
-            def _():
-                tile_copy(i, j, n).start()
-
-            return n + jnp.where(on, 1, 0)
-
-        live.append(lax.fori_loop(0, 2 * NZ, visit, 0))
+            far = lax.rem(z - lax.rem(j, NZ) + NZ, NZ)
+            slot = jnp.where(far == 0, 0, jnp.where(far <= NZ // 2, 2 * far - 1, 2 * (NZ - far)))
+            index[i, n] = (j // NZ) * NZ + slot
+            return n + jnp.where(mask[block, j] > 0, 1, 0)
+
+        n = lax.fori_loop(0, 2 * NZ, visit, 0)
+        for extra in range(TILES - 1):
+            index[i, n + extra] = 0
+        live.append(n)
 
     def chunks_of(n):
         return (n + TILES - 1) // TILES
 
-    for i in range(2):
-        n = live[i]
-        for extra in range(TILES - 1):
-            @pl.when(n + extra < chunks_of(n) * TILES)
-            def _():
-                kvc[i, n + extra] = jnp.zeros((BLK, WIDE), BF16)
-
     def keys_of(i, t):
-        return kvc[i, pl.ds(t * TILES, TILES)].reshape(CHUNK, WIDE)
+        return jnp.concatenate([keys_all[index[i, t * TILES + d]] for d in range(TILES)], axis=0)
 
     invs = []
     for i in range(2):
@@ -374,6 +367,22 @@
             qg[i, h * BLK : (h + 1) * BLK, :] = q[i * BLK : (i + 1) * BLK]
             qr[i, h * BLK : (h + 1) * BLK, :] = rope[i * BLK : (i + 1) * BLK]
 
+    def in_fours(count, step):
+        def four(t, _):
+            step(4 * t, 4)
+            return 0
+
+        lax.fori_loop(0, count // 4, four, 0)
+        rest = lax.rem(count, 4)
+
+        @pl.when(rest >= 2)
+        def _():
+            step(count - rest, 2)
+
+        @pl.when(lax.rem(rest, 2) == 1)
+        def _():
+            step(count - 1, 1)
+
     def in_pairs(count, step):
         def pair(t, _):
             step(2 * t, 2)
@@ -389,11 +398,8 @@
         n = live[i]
         count = chunks_of(n)
 
-        def arrived(t, _):
-            tile_copy(i, 0, t).wait()
-            return 0
-
-        lax.fori_loop(0, n, arrived, 0)
+        if i == 0:
+            loads[7].wait()
         peak[...] = jnp.full((rows, 128), LOWEST, F32)
         lsum[...] = jnp.zeros((rows, 128), F32)
         gsum[...] = jnp.zeros((rows, 128), F32)
@@ -436,10 +442,10 @@
             weight = jnp.concatenate(
                 [(sbuf[first + d] * (dbuf[first + d] - ratio)).astype(BF16) for d in range(many)], axis=1
             )
-            keys = kvc[i, pl.ds(first * TILES, many * TILES)].reshape(many * CHUNK, WIDE)
+            keys = jnp.concatenate([keys_of(i, first + d) for d in range(many)], axis=0)
             acc[...] += jnp.dot(weight, keys, preferred_element_type=F32)
 
-        in_pairs(count, collect)
+        in_fours(count, collect)
         grad = acc[...] * (scale / total)
         gl[i] = grad[:, :KVL].astype(BF16).reshape(HALF, BLK, KVL)
         gr[i] = grad[:, KVL:].reshape(HALF, BLK, WIDE - KVL)
@@ -487,7 +493,7 @@
             pltpu.VMEM((KVL, DCOLS), BF16),
             pltpu.VMEM((KVL, DCOLS), BF16),
             pltpu.VMEM((2, BLK, DCOLS), BF16),
-            pltpu.VMEM((2, 2 * NZ, BLK, WIDE), BF16),
+            pltpu.VMEM((2 * NZ, BLK, WIDE), BF16),
             pltpu.VMEM((2, BLK, ql), BF16),
             pltpu.VMEM((2 * BLK, QCOLS), F32),
             pltpu.VMEM((2, 2 * rows, KVL), BF16),
@@ -501,8 +507,8 @@
             pltpu.VMEM((rows, 128), F32),
             pltpu.VMEM((rows, 128), F32),
             pltpu.VMEM((16, QCOLS), F32),
-            pltpu.SemaphoreType.DMA((7,)),
-            pltpu.SemaphoreType.DMA((2, 2 * NZ)),
+            pltpu.SMEM((2, 2 * NZ + TILES), jnp.int32),
+            pltpu.SemaphoreType.DMA((8,)),
         ],
         compiler_params=pltpu.CompilerParams(vmem_limit_bytes=54 * 2**20),
         cost_estimate=pl.CostEstimate(flops=10_000_000_000, bytes_accessed=10_000_000, transcendentals=4_000_000),
@@ -510,47 +516,45 @@
     )(mask, q, xq, b, xb, gain, W, s, xs, KV, w_uk, w_uv, d, xd)
 
 
-def reduce_kernel(gs_ref, lb_ref, steer_out, bias_out, total, rbuf, rgs, rlb, p_s, p_r, g_s, g_r):
+def reduce_kernel(gs_ref, lb_ref, steer_out, bias_out, rbuf, rgs, p_s, p_r, g_s, g_r):
     c, k, a, z = place()
-    pair = ((1 - a) * NZ + z, k)
+    pair_c = (1 - a) * NZ + z
     n = 16
 
-    def mate(shift):
-        return (c, lax.rem(k + shift + n, n))
-
+    def mate(side, shift):
+        return (pair_c if side else c, lax.rem(k + shift, n))
+
+    others = [(side, shift) for side in range(2) for shift in range(n) if side or shift]
     barrier = pltpu.get_barrier_semaphore()
-    pl.semaphore_signal(barrier, inc=1, device_id=pair, device_id_type=MESH)
-    for shift in range(1, n):
-        pl.semaphore_signal(barrier, inc=1, device_id=mate(shift), device_id_type=MESH)
-    pl.semaphore_wait(barrier, n)
+    for one in others:
+        pl.semaphore_signal(barrier, inc=1, device_id=mate(*one), device_id_type=MESH)
+    pl.semaphore_wait(barrier, len(others))
 
     def copy(src, dst, s, r, dev):
         return pltpu.make_async_remote_copy(
             src_ref=src, dst_ref=dst, send_sem=s, recv_sem=r, device_id=dev, device_id_type=MESH
         )
 
-    first = copy(lb_ref.at[pl.ds(1, 1)], rlb, p_s.at[0], p_r.at[0], pair)
-    second = copy(gs_ref.at[pl.ds(1, 1)], rgs, p_s.at[1], p_r.at[1], pair)
-    first.start()
-    second.start()
-    first.wait_recv()
-    total[...] = lb_ref[0:1, :] + rlb[...]
+    steer_copy = copy(gs_ref.at[pl.ds(1, 1)], rgs, p_s.at[0], p_r.at[0], mate(1, 0))
+    steer_copy.start()
     out = []
-    for shift in range(1, n):
-        out.append(copy(total, rbuf.at[shift], g_s.at[shift], g_r.at[shift], mate(shift)))
+    for side, shift in others:
+        at = side * n + shift
+        out.append(
+            copy(lb_ref.at[pl.ds(side, 1)], rbuf.at[at], g_s.at[at], g_r.at[at], mate(side, shift))
+        )
         out[-1].start()
-    second.wait_recv()
+    steer_copy.wait_recv()
     mine = gs_ref[0:1, :]
     theirs = rgs[...]
     steer_out[:, :QCOLS] = jnp.where(a == 0, mine, theirs)
     steer_out[:, QCOLS:] = jnp.where(a == 0, theirs, mine)
-    result = total[...]
-    for shift in range(1, n):
-        out[shift - 1].wait_recv()
-        result = result + rbuf[shift]
+    result = lb_ref[0:1, :]
+    for (side, shift), one in zip(others, out):
+        one.wait_recv()
+        result = result + rbuf[side * n + shift]
     bias_out[...] = result
-    first.wait_send()
-    second.wait_send()
+    steer_copy.wait_send()
     for one in out:
         one.wait_send()
 
@@ -563,14 +567,12 @@
         in_specs=[VM, VM],
         out_specs=[VM, VM],
         scratch_shapes=[
-            pltpu.VMEM((1, ql), F32),
-            pltpu.VMEM((16, 1, ql), F32),
+            pltpu.VMEM((32, 1, ql), F32),
             pltpu.VMEM((1, QCOLS), F32),
-            pltpu.VMEM((1, ql), F32),
-            pltpu.SemaphoreType.DMA((2,)),
-            pltpu.SemaphoreType.DMA((2,)),
-            pltpu.SemaphoreType.DMA((16,)),
-            pltpu.SemaphoreType.DMA((16,)),
+            pltpu.SemaphoreType.DMA((1,)),
+            pltpu.SemaphoreType.DMA((1,)),
+            pltpu.SemaphoreType.DMA((32,)),
+            pltpu.SemaphoreType.DMA((32,)),
         ],
         compiler_params=pltpu.CompilerParams(collective_id=1, has_side_effects=True),
         name="reduce",
@@ -581,10 +583,10 @@
     q_latent, latent_bias, norm_gain, w_q, steer, kv_latent, key_rope, w_uk, w_uv, d_out, block_mask
 ):
     ql = q_latent.shape[1]
-    W, KV, Xq, Xb, Xs, Xd = gather(w_q, q_latent, latent_bias, steer, d_out, kv_latent, key_rope)
+    W, KV, Xq, Xb, Xs, Xd = gather(w_q, q_latent, latent_bias, steer, d_out, kv_latent, key_rope.T)
     gs, lb = attend(
         block_mask, q_latent, Xq, latent_bias, Xb, norm_gain, W.reshape(2, ql, QTWO), steer, Xs,
-        KV, w_uk, w_uv, d_out, Xd,
+        KV.reshape(2 * NZ, BLK, WIDE), w_uk, w_uv, d_out, Xd,
     )
     grad_steer, grad_bias = reduce(gs, lb)
     return (grad_steer, grad_bias)

time: 96.6 us -> 88.3 us (0.914)
  the two profiles are of different devices: /device:TPU:35 before, /device:TPU:131 now
where the time goes in v2:
time: 88.3 us; the launch traced here: 87.8 us
  Pallas kernels  84.6 us (96%)
  local copies, waits for them, and re-layouts  2.57 us (3%)
    pallas_call x1, Pallas kernels, gather(): pl.pallas_call(gather_kernel, out_shape=(jax.ShapeDtypeStruct((2, 2 * NZ,...  50 us
    pallas_call x1, Pallas kernels, attend(): pl.pallas_call(attend_kernel, out_shape=(jax.ShapeDtypeStruct((2, QCOLS),...  21.3 us
    pallas_call x1, Pallas kernels, reduce(): pl.pallas_call(reduce_kernel, out_shape=(jax.ShapeDtypeStruct((1, 2 * QCO...  13.3 us
    unnamed x2, local copies, waits for them, and re-layouts  2.57 us

profile of v2, /device:TPU:131, one launch (start us, length us, event | category | flops | bytes accessed | tf_op | source)
XLA Modules:
  0.0 87.8 jit_solution(2006123042381647137)
XLA Ops:
  0.6 50.0 %gather.1 = (bf16[2,32,48,384]{3,2,1,0:T(8,128)(2,1)}, bf16[2,16,128,640]{3,2,1,0:T(8,128)(2,1)}, bf16[128,1536]{1,0:T(8,128)(2,1)}, f32[1,1536]{1,0:T(1,128)}, ...) custom-call(bf16[48,1536]{1,0:T(8,128)(2,1)} %w_ref.1, bf16[128,1536]{1,0:T(8,128)(2,1)} %q_ref.3, f32[1,1536]{1,0:T(1,128)} %b_ref.3, ...), custom_call_target="tpu_custom_call" | custom-call | bytes 20000000 | tf_op jit(solution)/shard_map/gather/pallas_call | solution.py:258
  50.6 21.3 %attend.1 = (f32[2,768]{1,0:T(2,128)}, f32[2,1536]{1,0:T(2,128)}) custom-call(s32[32,32]{1,0:T(8,128)} %mask.1, bf16[128,1536]{1,0:T(8,128)(2,1)} %q_ref.3, bf16[128,1536]{1,0:T(8,128)(2,1)} %get-tuple-element.10.xq_ref, f32[1,1536]{1,0:T(1,128)} %b_ref.3, f32[1,1536]{1,0:T(1,128)} %get-tuple-element.11.xb_ref, f32[1536]{0:T(1024)} %gain_ref.1, ...), custom_call_target="tpu_custom_call" | custom-call | flops 10000000000 | bytes 10000000 | tf_op jit(solution)/shard_map/attend/pallas_call | solution.py:483
  71.9 13.3 %reduce.1 = (f32[1,1536]{1,0:T(1,128)}, f32[1,1536]{1,0:T(1,128)}) custom-call(f32[2,768]{1,0:T(2,128)} %get-tuple-element.16.gs_ref, f32[2,1536]{1,0:T(2,128)} %get-tuple-element.17.lb_ref), custom_call_target="tpu_custom_call" | custom-call | tf_op jit(solution)/shard_map/reduce/pallas_call | solution.py:564
  85.2 1.3 %copy.15 = f32[1,1536]{1,0:T(1,128)} copy(f32[1,1536]{1,0:T(1,128)} %get-tuple-element.20) | data formatting | bytes 12288
  86.5 1.3 %copy.16 = f32[1,1536]{1,0:T(1,128)} copy(f32[1,1536]{1,0:T(1,128)} %get-tuple-element.21) | data formatting | bytes 12288

commit v3 on v2

v3 whole, which is shorter than its diff:
```python
import functools
import math

import jax
import jax.numpy as jnp
from jax import lax
from jax.experimental import pallas as pl
from jax.experimental.pallas import tpu as pltpu
from jax.sharding import PartitionSpec as P

KVL = 512
NOPE = 128
ROPE = 64
BLK = 128
WIDE = 640
HALF = 4
HEADW = NOPE + ROPE
QCOLS = HALF * HEADW
QTWO = QCOLS // 2
DCOLS = HALF * NOPE
EPS = 1e-06
LOWEST = -1e30
NZ = 16
NY = 4
MESH = pl.DeviceIdType.MESH
F32 = jnp.float32
BF16 = jnp.bfloat16
ANY = pl.BlockSpec(memory_space=pl.ANY)
HBM = pl.BlockSpec(memory_space=pltpu.HBM)
VM = pl.BlockSpec(memory_space=pltpu.VMEM)


def last_last(left, right):
    return lax.dot_general(left, right, (((1,), (1,)), ((), ())), preferred_element_type=F32)


def place():
    c = lax.axis_index("ctx")
    k = lax.axis_index("head")
    return c, k, c // NZ, lax.rem(c, NZ)


def gather_kernel(
    w_ref, q_ref, b_ref, s_ref, d_ref, kv_ref, kr_ref, uk_ref, uv_ref, gain_ref,
    W_out, KV_out, xq_out, xb_out, qg_out, qr_out, pj_out,
    qg, qr, pj, W, KV, own, rope, q2, bv, sv, dv, uk, uv, cq,
    w_s, w_r, z_s, z_r, y_s, y_r, f_s, f_r, x_s, x_r, c_s, c_r, m_s, m_r, loc, fill, drain,
):
    c, k, a, z = place()
    x_hi = k // 8
    y = lax.rem(k, 8) // 2
    core = lax.rem(k, 2)
    z_right = (a * NZ + lax.rem(z + 1, NZ), k)
    z_left = (a * NZ + lax.rem(z + NZ - 1, NZ), k)
    first_hop = 2 - x_hi
    z_first = tuple((a * NZ + lax.rem(z + NZ + way * first_hop, NZ), k) for way in (1, -1))
    z_next = tuple((a * NZ + lax.rem(z + NZ + way * 2, NZ), k) for way in (1, -1))
    y_right = (c, x_hi * 8 + lax.rem(y + 1, NY) * 2 + core)
    y_left = (c, x_hi * 8 + lax.rem(y + NY - 1, NY) * 2 + core)
    sibling = (c, x_hi * 8 + y * 2 + (1 - core))
    pair = ((1 - a) * NZ + z, k)
    across = ((1 - a) * NZ + z, (1 - x_hi) * 8 + y * 2 + core)
    far = (c, (1 - x_hi) * 8 + y * 2 + core)

    barrier = pltpu.get_barrier_semaphore()
    for dev in (z_right, z_left, *z_first, *z_next, y_right, y_left, sibling, pair, across, far):
        pl.semaphore_signal(barrier, inc=1, device_id=dev, device_id_type=MESH)

    my_d = pl.ds(pl.multiple_of(a * DCOLS, 128), DCOLS)
    fills = [
        pltpu.make_async_copy(q_ref, q2.at[0], fill.at[0]),
        pltpu.make_async_copy(b_ref, bv.at[0], fill.at[1]),
        pltpu.make_async_copy(s_ref, sv.at[0], fill.at[2]),
        pltpu.make_async_copy(d_ref.at[:, my_d], dv.at[0], fill.at[3]),
        pltpu.make_async_copy(uk_ref.at[:, my_d], uk, fill.at[4]),
        pltpu.make_async_copy(uv_ref.at[:, my_d], uv, fill.at[5]),
    ]
    load_k = pltpu.make_async_copy(kv_ref, own.at[:, pl.ds(0, KVL)], loc.at[2])
    load_r = pltpu.make_async_copy(kr_ref, rope, loc.at[3])
    load_k.start()
    load_r.start()
    load_r.wait()
    tall = jnp.concatenate([rope[...].astype(F32), jnp.zeros((WIDE - KVL - ROPE, BLK), F32)], axis=0)
    own[:, KVL:] = tall.T.astype(BF16)
    load_k.wait()
    for copy in fills:
        copy.start()
    pl.semaphore_wait(barrier, 12)

    sends = []

    def send(src, dst, s, r, dev):
        copy = pltpu.make_async_remote_copy(
            src_ref=src, dst_ref=dst, send_sem=s, recv_sem=r, device_id=dev, device_id_type=MESH
        )
        copy.start()
        sends.append(copy)

    def got(dst, s, r):
        pltpu.make_async_remote_copy(
            src_ref=dst, dst_ref=dst, send_sem=s, recv_sem=r, device_id=pair, device_id_type=MESH
        ).wait_recv()

    def columns(who, two):
        return pl.ds(pl.multiple_of(who * QCOLS + two * QTWO, 128), QTWO)

    their_d = pl.ds(pl.multiple_of((1 - a) * DCOLS, 128), DCOLS)

    counts = {(0, 0): 8, (0, 1): 7, (1, 0): 7, (1, 1): 8}

    def w_slot(part, two, zz):
        return W.at[two, (a if part == 0 else 1 - a) * NZ + lax.rem(zz + 2 * NZ, NZ)]

    def w_send(way, part, two, step):
        at = z - (step - 1) if way == 0 else z + (step - 1)
        slot = w_slot(part, two, at)
        src = w_ref.at[:, columns(a, two)] if step == 1 and part == 0 else slot
        n = 4 * way + 2 * part + two
        send(src, slot, w_s.at[n, step - 1], w_r.at[n, step - 1], z_left if way else z_right)

    def w(step):
        for part, two in ((0, 0), (0, 1), (1, 0), (1, 1)):
            for way in (0, 1):
                if step <= counts[way, part]:
                    n = 4 * way + 2 * part + two
                    at = z + step if way else z - step
                    got(w_slot(part, two, at), w_s.at[n, step - 1], w_r.at[n, step - 1])
                    if step + 1 <= counts[way, part]:
                        w_send(way, part, two, step + 1)

    rows = pl.ds(pl.multiple_of(core * 64 + y * 16, 16), 16)

    def z_slot(way, step):
        at = jnp.where(x_hi == 0, 2 * step - 1, 2 * step - 2) + way
        return KV.at[at // 2, a, x_hi, lax.rem(at, 2), rows]

    def z_send(way, step):
        src = own.at[rows] if step == 1 else z_slot(way, step - 1)
        dev = (z_first if step == 1 else z_next)[way]
        send(src, z_slot(way, step), z_s.at[way, step - 1], z_r.at[way, step - 1], dev)

    def kz(step):
        def one(way):
            got(z_slot(way, step), z_s.at[way, step - 1], z_r.at[way, step - 1])

        one(0)
        if step < 4:
            z_send(0, step + 1)
            one(1)
            if step < 3:
                z_send(1, step + 1)
            else:
                pl.when(x_hi == 1)(lambda: last_left().start())
        else:
            pl.when(x_hi == 1)(lambda: one(1))

    def last_left():
        return pltpu.make_async_remote_copy(
            src_ref=KV.at[2, a, 1, 1, rows], dst_ref=KV.at[3, a, 1, 1, rows],
            send_sem=z_s.at[1, 3], recv_sem=z_r.at[1, 3], device_id=z_next[1], device_id_type=MESH,
        )

    def y_rows(shift):
        return pl.ds(pl.multiple_of(core * 64 + lax.rem(y + shift + NY, NY) * 16, 16), 16)

    def kx(q):
        part = KV.at[q, a, x_hi, :, rows]
        for n, dev in ((0, far), (1, across), (2, pair)):
            send(part, part, x_s.at[n, q], x_r.at[n, q], dev)

    def ky(q):
        for n, side, parity in ((2, 1 - a, x_hi), (1, 1 - a, 1 - x_hi), (0, a, 1 - x_hi)):
            got(KV.at[q, side, parity, :, rows], x_s.at[n, q], x_r.at[n, q])
        part = KV.at[q, :, :, :, rows]
        for way in range(2):
            send(part, part, y_s.at[way, q], y_r.at[way, q], y_left if way else y_right)

    def kf(q):
        for way in range(2):
            row = y_rows(1 if way else -1)
            got(KV.at[q, :, :, :, row], y_s.at[way, q], y_r.at[way, q])
            part = KV.at[q, way, :, :, row]
            send(part, part, f_s.at[way, q], f_r.at[way, q], y_left if way else y_right)

    half = pl.ds(pl.multiple_of(core * 64, 16), 64)

    def kc(q):
        for way in range(2):
            got(KV.at[q, way, :, :, y_rows(2)], f_s.at[way, q], f_r.at[way, q])
        part = KV.at[q, :, :, :, half]
        send(part, part, c_s.at[q], c_r.at[q], sibling)

    for two in range(2):
        send(w_ref.at[:, columns(1 - a, two)], W.at[two, c], m_s.at[6 * two], m_r.at[6 * two], pair)
    z_send(0, 1)
    z_send(1, 1)
    for two in range(2):
        w_send(0, 0, two, 1)
        w_send(1, 0, two, 1)
    copy_w = [pltpu.make_async_copy(w_ref.at[:, columns(a, two)], W.at[two, c], loc.at[4 * two]) for two in range(2)]
    for copy in copy_w:
        copy.start()
    copy_k = pltpu.make_async_copy(own.at[rows], KV.at[0, a, 0, 0, rows], loc.at[1])
    pl.when(x_hi == 0)(lambda: copy_k.start())
    q_rows = pl.ds(pl.multiple_of(core * 64, 16), 64)
    send(q_ref.at[q_rows], q2.at[1, q_rows], m_s.at[1], m_r.at[1], pair)
    send(d_ref.at[:, their_d], dv.at[1], m_s.at[3], m_r.at[3], pair)
    send(b_ref, bv.at[1], m_s.at[4], m_r.at[4], pair)
    send(s_ref, sv.at[1], m_s.at[5], m_r.at[5], pair)
    for two in range(2):
        got(w_slot(1, two, z), m_s.at[6 * two], m_r.at[6 * two])
        w_send(0, 1, two, 1)
        w_send(1, 1, two, 1)

    both = 2 * BLK
    gain = gain_ref[...].reshape(1, gain_ref.shape[0])

    def norm(i):
        shifted = q2[i].astype(F32) + bv[i]
        inv = lax.rsqrt(jnp.mean(shifted * shifted, axis=1, keepdims=True) + EPS)
        cq[i] = (shifted * inv * gain).astype(BF16)

    def absorb_g(i):
        for h in range(HALF):
            up = slice(h * NOPE, (h + 1) * NOPE)
            qg[i, (HALF + h) * BLK : (HALF + h + 1) * BLK, :] = last_last(dv[i, :, up], uv[:, up]).astype(BF16)

    other = pl.ds(pl.multiple_of((1 - core) * 64, 16), 64)
    drains = []

    def store(src, dst):
        drains.append(pltpu.make_async_copy(src, dst, drain.at[len(drains)]))
        drains[-1].start()

    def kend(q):
        got(KV.at[q, :, :, :, other], c_s.at[q], c_r.at[q])
        store(KV.at[q], KV_out.at[q])

    for copy in fills:
        copy.wait()
    norm(0)
    kz(1)
    pl.when(x_hi == 0)(lambda: copy_k.wait())
    kx(0)
    w(1)
    absorb_g(0)
    kz(2)
    kx(1)
    ky(0)
    w(2)
    kz(3)
    kx(2)
    kf(0)
    ky(1)
    got(q2.at[1, q_rows], m_s.at[1], m_r.at[1])
    send(q2.at[1, q_rows], q2.at[1, q_rows], m_s.at[2], m_r.at[2], sibling)
    w(3)
    kz(4)
    kx(3)
    kf(1)
    ky(2)
    kc(0)
    w(4)
    got(q2.at[1, other], m_s.at[2], m_r.at[2])
    got(dv.at[1], m_s.at[3], m_r.at[3])
    got(bv.at[1], m_s.at[4], m_r.at[4])
    got(sv.at[1], m_s.at[5], m_r.at[5])
    store(q2.at[1], xq_out)
    store(bv.at[1], xb_out)
    norm(1)
    ky(3)
    kf(2)
    kc(1)
    w(5)
    absorb_g(1)
    store(qg.at[:, pl.ds(HALF * BLK, HALF * BLK)], qg_out.at[:, pl.ds(HALF * BLK, HALF * BLK)])
    kend(0)
    kf(3)
    w(6)
    kc(2)
    kend(1)
    w(7)
    kc(3)
    kend(2)
    w(8)
    kend(3)
    for copy in copy_w:
        copy.wait()
    store(W, W_out)
    c_query = cq[...].reshape(both, cq.shape[2])
    for two in range(2):
        weights = W[two].reshape(cq.shape[2], QTWO)
        proj = jnp.dot(c_query, weights, preferred_element_type=F32)
        pj[two] = proj
        store(pj.at[two], pj_out.at[two])
        query = []
        for i in range(2):
            row = sv[i]
            part = slice(two * QTWO, (two + 1) * QTWO)
            rest = slice(QCOLS + two * QTWO, QCOLS + (two + 1) * QTWO)
            query.append(proj[i * BLK : (i + 1) * BLK] + jnp.where(a == 0, row[:, part], row[:, rest]))
        query = jnp.concatenate(query, axis=0).astype(BF16)
        for local in range(2):
            h = 2 * two + local
            at = local * HEADW
            q = last_last(query[:, at : at + NOPE], uk[:, h * NOPE : (h + 1) * NOPE]).astype(BF16)
            pos = query[:, at + NOPE : at + HEADW]
            pos = jnp.concatenate([pos, jnp.zeros((both, WIDE - KVL - ROPE), BF16)], axis=1)
            for i in range(2):
                qg[i, h * BLK : (h + 1) * BLK, :] = q[i * BLK : (i + 1) * BLK]
                qr[i, h * BLK : (h + 1) * BLK, :] = pos[i * BLK : (i + 1) * BLK]
        done = pl.ds(2 * two * BLK, 2 * BLK)
        store(qg.at[:, done], qg_out.at[:, done])
    store(qr, qr_out)
    for copy in drains:
        copy.wait()
    pl.when(x_hi == 1)(lambda: last_left().wait_send())
    for copy in sends:
        copy.wait_send()


def gather(w_q, q_latent, latent_bias, steer, d_out, kv_latent, key_rope, w_uk, w_uv, gain):
    def dma(*shape):
        return pltpu.SemaphoreType.DMA(shape)

    ql = q_latent.shape[1]
    rows = HALF * BLK
    w_shape = (2, 2 * NZ, w_q.shape[0], QTWO)
    k_shape = (NZ // 4, 2, 2, 2, BLK, WIDE)
    return pl.pallas_call(
        gather_kernel,
        out_shape=(
            jax.ShapeDtypeStruct(w_shape, BF16),
            jax.ShapeDtypeStruct(k_shape, BF16),
            jax.ShapeDtypeStruct(q_latent.shape, BF16),
            jax.ShapeDtypeStruct(latent_bias.shape, F32),
            jax.ShapeDtypeStruct((2, 2 * rows, KVL), BF16),
            jax.ShapeDtypeStruct((2, rows, WIDE - KVL), BF16),
            jax.ShapeDtypeStruct((2, 2 * BLK, QTWO), F32),
        ),
        in_specs=[HBM] * 9 + [VM],
        out_specs=[HBM] * 7,
        scratch_shapes=[
            pltpu.VMEM((2, 2 * rows, KVL), BF16),
            pltpu.VMEM((2, rows, WIDE - KVL), BF16),
            pltpu.VMEM((2, 2 * BLK, QTWO), F32),
            pltpu.VMEM(w_shape, BF16),
            pltpu.VMEM(k_shape, BF16),
            pltpu.VMEM((BLK, WIDE), BF16),
            pltpu.VMEM((ROPE, BLK), BF16),
            pltpu.VMEM((2, BLK, ql), BF16),
            pltpu.VMEM((2, 1, ql), F32),
            pltpu.VMEM((2, 1, 2 * QCOLS), F32),
            pltpu.VMEM((2, BLK, DCOLS), BF16),
            pltpu.VMEM((KVL, DCOLS), BF16),
            pltpu.VMEM((KVL, DCOLS), BF16),
            pltpu.VMEM((2, BLK, ql), BF16),
            dma(8, 8), dma(8, 8), dma(2, 4), dma(2, 4), dma(2, 4), dma(2, 4), dma(2, 4), dma(2, 4),
            dma(3, 4), dma(3, 4), dma(4), dma(4), dma(7), dma(7), dma(5), dma(6), dma(16),
        ],
        compiler_params=pltpu.CompilerParams(
            collective_id=0, has_side_effects=True, vmem_limit_bytes=54 * 2**20
        ),
        cost_estimate=pl.CostEstimate(flops=2_000_000_000, bytes_accessed=20_000_000, transcendentals=0),
        name="gather",
    )(w_q, q_latent, latent_bias, steer, d_out, kv_latent, key_rope, w_uk, w_uv, gain)


CHUNK = 256
TILES = CHUNK // BLK


def attend_kernel(
    mask, qg_ref, qr_ref, KV, gl, gr, keys_all, qg, qr, sbuf, dbuf, acc, peak, lsum, gsum, index, sem
):
    c, k, a, z = place()
    scale = HEADW ** (-0.5)
    scale2 = scale * math.log2(math.e)
    rows = HALF * BLK
    loads = [
        pltpu.make_async_copy(qg_ref.at[0], qg.at[0], sem.at[0]),
        pltpu.make_async_copy(qr_ref, qr, sem.at[1]),
        pltpu.make_async_copy(KV, keys_all, sem.at[2]),
        pltpu.make_async_copy(qg_ref.at[1], qg.at[1], sem.at[3]),
    ]
    for copy in loads:
        copy.start()

    live = []
    for i in range(2):
        block = c if i == 0 else lax.rem(c + NZ, 2 * NZ)

        def visit(j, n):
            away = lax.rem(z - lax.rem(j, NZ) + NZ, NZ)
            left = away > NZ // 2
            hops = jnp.where(left, NZ - away, away)
            slot = jnp.where(away == 0, 0, jnp.where(left, hops, hops - 1))
            index[i, n] = ((slot // 2 * 2 + j // NZ) * 2 + lax.rem(hops, 2)) * 2 + lax.rem(slot, 2)
            return n + jnp.where(mask[block, j] > 0, 1, 0)

        n = lax.fori_loop(0, 2 * NZ, visit, 0)
        for extra in range(TILES - 1):
            index[i, n + extra] = 0
        live.append(n)

    def chunks_of(n):
        return (n + TILES - 1) // TILES

    def keys_of(i, t):
        return jnp.concatenate([keys_all[index[i, t * TILES + d]] for d in range(TILES)], axis=0)

    def in_fours(count, step):
        def four(t, _):
            step(4 * t, 4)
            return 0

        lax.fori_loop(0, count // 4, four, 0)
        rest = lax.rem(count, 4)

        @pl.when(rest >= 2)
        def _():
            step(count - rest, 2)

        @pl.when(lax.rem(rest, 2) == 1)
        def _():
            step(count - 1, 1)

    def in_pairs(count, step):
        def pair(t, _):
            step(2 * t, 2)
            return 0

        lax.fori_loop(0, count // 2, pair, 0)

        @pl.when(lax.rem(count, 2) == 1)
        def _():
            step(count - 1, 1)

    for i in range(2):
        n = live[i]
        count = chunks_of(n)

        for copy in loads[3 * i : 3 * i + 3]:
            copy.wait()
        peak[...] = jnp.full((rows, 128), LOWEST, F32)
        lsum[...] = jnp.zeros((rows, 128), F32)
        gsum[...] = jnp.zeros((rows, 128), F32)
        acc[...] = jnp.zeros((rows, WIDE), F32)

        def scores(first, many):
            top = peak[...]
            for t in [first + d for d in range(many)]:
                keys = keys_of(i, t)
                column = lax.broadcasted_iota(jnp.int32, (1, CHUNK), 1) + t * CHUNK
                dead = jnp.where(column < n * BLK, 0.0, LOWEST)
                main = last_last(qg[i], keys[:, :KVL])
                s = main[:rows] + last_last(qr[i], keys[:, KVL:]) + dead
                sbuf[t] = s
                dbuf[t] = main[rows:]
                for part in range(TILES):
                    top = jnp.maximum(top, s[:, part * 128 : (part + 1) * 128])
            peak[...] = top

        in_pairs(count, scores)
        top = jnp.max(peak[...], axis=1, keepdims=True) * scale2

        def weigh(first, many):
            low = lsum[...]
            gow = gsum[...]
            for t in [first + d for d in range(many)]:
                e = jnp.exp2(sbuf[t] * scale2 - top)
                sbuf[t] = e
                mixed = e * dbuf[t]
                low = low + sum(e[:, p * 128 : (p + 1) * 128] for p in range(TILES))
                gow = gow + sum(mixed[:, p * 128 : (p + 1) * 128] for p in range(TILES))
            lsum[...] = low
            gsum[...] = gow

        in_pairs(count, weigh)
        total = jnp.sum(lsum[...], axis=1, keepdims=True)
        ratio = jnp.sum(gsum[...], axis=1, keepdims=True) / total

        def collect(first, many):
            weight = jnp.concatenate(
                [(sbuf[first + d] * (dbuf[first + d] - ratio)).astype(BF16) for d in range(many)], axis=1
            )
            keys = jnp.concatenate([keys_of(i, first + d) for d in range(many)], axis=0)
            acc[...] += jnp.dot(weight, keys, preferred_element_type=F32)

        in_fours(count, collect)
        grad = acc[...] * (scale / total)
        gl[i] = grad[:, :KVL].astype(BF16).reshape(HALF, BLK, KVL)
        gr[i] = grad[:, KVL:].reshape(HALF, BLK, WIDE - KVL)


def attend(mask, qg, qr, KV):
    rows = HALF * BLK
    nchunk = 2 * NZ // TILES
    return pl.pallas_call(
        attend_kernel,
        out_shape=(
            jax.ShapeDtypeStruct((2, HALF, BLK, KVL), BF16),
            jax.ShapeDtypeStruct((2, HALF, BLK, WIDE - KVL), F32),
        ),
        in_specs=[pl.BlockSpec(memory_space=pltpu.SMEM), HBM, HBM, HBM],
        out_specs=[VM, VM],
        scratch_shapes=[
            pltpu.VMEM((2 * NZ, BLK, WIDE), BF16),
            pltpu.VMEM((2, 2 * rows, KVL), BF16),
            pltpu.VMEM((2, rows, WIDE - KVL), BF16),
            pltpu.VMEM((nchunk, rows, CHUNK), F32),
            pltpu.VMEM((nchunk, rows, CHUNK), F32),
            pltpu.VMEM((rows, WIDE), F32),
            pltpu.VMEM((rows, 128), F32),
            pltpu.VMEM((rows, 128), F32),
            pltpu.VMEM((rows, 128), F32),
            pltpu.SMEM((2, 2 * NZ + TILES), jnp.int32),
            pltpu.SemaphoreType.DMA((4,)),
        ],
        compiler_params=pltpu.CompilerParams(vmem_limit_bytes=54 * 2**20),
        cost_estimate=pl.CostEstimate(flops=10_000_000_000, bytes_accessed=10_000_000, transcendentals=4_000_000),
        name="attend",
    )(mask, qg, qr, KV)


def reduce_kernel(
    q_ref, xq_ref, b_ref, xb_ref, gain_ref, W_ref, uk_ref, pj_ref, gl_ref, gr_ref,
    steer_out, bias_out,
    q2, Wv, uk, pj, gl, gr, u_ref, gs_ref, lb_ref, rbuf, rgs, p_s, p_r, g_s, g_r, sem,
):
    c, k, a, z = place()
    pair_c = (1 - a) * NZ + z
    n = 16

    def mate(side, shift):
        return (pair_c if side else c, lax.rem(k + shift, n))

    my_d = pl.ds(pl.multiple_of(a * DCOLS, 128), DCOLS)
    loads = [
        pltpu.make_async_copy(gl_ref, gl, sem.at[0]),
        pltpu.make_async_copy(uk_ref.at[:, my_d], uk, sem.at[1]),
        pltpu.make_async_copy(gr_ref, gr, sem.at[2]),
        pltpu.make_async_copy(pj_ref, pj, sem.at[3]),
        pltpu.make_async_copy(q_ref, q2.at[0], sem.at[4]),
        pltpu.make_async_copy(xq_ref, q2.at[1], sem.at[5]),
        pltpu.make_async_copy(W_ref, Wv, sem.at[6]),
    ]
    for load in loads:
        load.start()
    others = [(side, shift) for side in range(2) for shift in range(n) if side or shift]
    barrier = pltpu.get_barrier_semaphore()
    for one in others:
        pl.semaphore_signal(barrier, inc=1, device_id=mate(*one), device_id_type=MESH)
    both = 2 * BLK
    gain = gain_ref[...].reshape(1, gain_ref.shape[0])
    for load in loads:
        load.wait()
    pieces = []
    for h in range(HALF):
        pieces.append(
            jnp.dot(gl[:, h].reshape(both, KVL), uk[:, h * NOPE : (h + 1) * NOPE], preferred_element_type=F32)
        )
        pieces.append(gr[:, h].reshape(both, WIDE - KVL)[:, :ROPE])
    all_grads = jnp.concatenate(pieces, axis=1)
    u_ref[...] = jnp.zeros_like(u_ref)
    for i in range(2):
        shifted = q2[i].astype(F32) + (b_ref, xb_ref)[i][...]
        inv = lax.rsqrt(jnp.mean(shifted * shifted, axis=1, keepdims=True) + EPS)
        grad_query = all_grads[i * BLK : (i + 1) * BLK]
        gs_ref[i : i + 1, :] = jnp.sum(grad_query, axis=0, keepdims=True)
        lean = sum(
            jnp.sum(
                grad_query[:, two * QTWO : (two + 1) * QTWO] * pj[two, i * BLK : (i + 1) * BLK, :], axis=1, keepdims=True
            )
            for two in range(2)
        )
        u = jnp.sum(grad_query * inv, axis=0, keepdims=True)
        u_high = u.astype(BF16)
        u_ref[2 * i : 2 * i + 1, :] = u_high.astype(F32)
        u_ref[2 * i + 1 : 2 * i + 2, :] = u - u_high.astype(F32)
        lb_ref[i : i + 1, :] = jnp.sum(shifted * (inv * inv * lean), axis=0, keepdims=True)

    back = sum(
        last_last(u_ref[:, two * QTWO : (two + 1) * QTWO].astype(BF16), Wv[two]) for two in range(2)
    )
    for i in range(2):
        whole = back[2 * i : 2 * i + 1] + back[2 * i + 1 : 2 * i + 2]
        lb_ref[i : i + 1, :] = gain * whole - lb_ref[i : i + 1, :] * (1.0 / gain.shape[1])
    pl.semaphore_wait(barrier, len(others))

    def copy(src, dst, s, r, dev):
        return pltpu.make_async_remote_copy(
            src_ref=src, dst_ref=dst, send_sem=s, recv_sem=r, device_id=dev, device_id_type=MESH
        )

    steer_copy = copy(gs_ref.at[pl.ds(1, 1)], rgs, p_s.at[0], p_r.at[0], mate(1, 0))
    steer_copy.start()
    out = []
    for side, shift in others:
        at = side * n + shift
        out.append(
            copy(lb_ref.at[pl.ds(side, 1)], rbuf.at[at], g_s.at[at], g_r.at[at], mate(side, shift))
        )
        out[-1].start()
    steer_copy.wait_recv()
    mine = gs_ref[0:1, :]
    theirs = rgs[...]
    steer_out[:, :QCOLS] = jnp.where(a == 0, mine, theirs)
    steer_out[:, QCOLS:] = jnp.where(a == 0, theirs, mine)
    result = lb_ref[0:1, :]
    for (side, shift), one in zip(others, out):
        one.wait_recv()
        result = result + rbuf[side * n + shift]
    bias_out[...] = result
    steer_copy.wait_send()
    for one in out:
        one.wait_send()


def reduce(q, xq, b, xb, gain, W, w_uk, pj, gl, gr):
    ql = q.shape[1]
    return pl.pallas_call(
        reduce_kernel,
        out_shape=(jax.ShapeDtypeStruct((1, 2 * QCOLS), F32), jax.ShapeDtypeStruct((1, ql), F32)),
        in_specs=[HBM, HBM, VM, VM, VM, HBM, HBM, HBM, HBM, HBM],
        out_specs=[VM, VM],
        scratch_shapes=[
            pltpu.VMEM((2, BLK, ql), BF16),
            pltpu.VMEM((2, ql, QTWO), BF16),
            pltpu.VMEM((KVL, DCOLS), BF16),
            pltpu.VMEM((2, 2 * BLK, QTWO), F32),
            pltpu.VMEM((2, HALF, BLK, KVL), BF16),
            pltpu.VMEM((2, HALF, BLK, WIDE - KVL), F32),
            pltpu.VMEM((16, QCOLS), F32),
            pltpu.VMEM((2, QCOLS), F32),
            pltpu.VMEM((2, ql), F32),
            pltpu.VMEM((32, 1, ql), F32),
            pltpu.VMEM((1, QCOLS), F32),
            pltpu.SemaphoreType.DMA((1,)),
            pltpu.SemaphoreType.DMA((1,)),
            pltpu.SemaphoreType.DMA((32,)),
            pltpu.SemaphoreType.DMA((32,)),
            pltpu.SemaphoreType.DMA((7,)),
        ],
        compiler_params=pltpu.CompilerParams(
            collective_id=1, has_side_effects=True, vmem_limit_bytes=54 * 2**20
        ),
        name="reduce",
    )(q, xq, b, xb, gain, W, w_uk, pj, gl, gr)


def shards(
    q_latent, latent_bias, norm_gain, w_q, steer, kv_latent, key_rope, w_uk, w_uv, d_out, block_mask
):
    ql = q_latent.shape[1]
    W, KV, xq, xb, qg, qr, pj = gather(
        w_q, q_latent, latent_bias, steer, d_out, kv_latent, key_rope.T, w_uk, w_uv, norm_gain
    )
    gl, gr = attend(block_mask, qg, qr, KV.reshape(2 * NZ, BLK, WIDE))
    grad_steer, grad_bias = reduce(
        q_latent, xq, latent_bias, xb, norm_gain, W.reshape(2, ql, QTWO), w_uk, pj, gl, gr
    )
    return (grad_steer, grad_bias)


def solution(mesh):
    in_specs = (
        P("ctx", None),
        P("ctx", None),
        P(),
        P("ctx", "head"),
        P("ctx", "head"),
        P("ctx", None),
        P("ctx", None),
        P(None, "head"),
        P(None, "head"),
        P("ctx", "head"),
        P(),
    )
    out_specs = (P("ctx", "head"), P("ctx", None))
    return jax.shard_map(shards, mesh=mesh, in_specs=in_specs, out_specs=out_specs, check_vma=False)
```

time: 88.3 us -> 97.3 us (1.10)
  the two profiles are of different devices: /device:TPU:131 before, /device:TPU:1 now
where the time goes in v3:
time: 97.3 us; the launch traced here: 96.7 us
  Pallas kernels  93.5 us (96%)
  local copies, waits for them, and re-layouts  2.57 us (3%)
    pallas_call x1, Pallas kernels, gather(): pl.pallas_call(gather_kernel, out_shape=(jax.ShapeDtypeStruct(w_shape, BF...  63.4 us
    pallas_call x1, Pallas kernels, attend(): pl.pallas_call(attend_kernel, out_shape=(jax.ShapeDtypeStruct((2, HALF, B...  16.8 us
    pallas_call x1, Pallas kernels, reduce(): pl.pallas_call(reduce_kernel, out_shape=(jax.ShapeDtypeStruct((1, 2 * QCO...  13.2 us
    unnamed x2, local copies, waits for them, and re-layouts  2.57 us

profile of v3, /device:TPU:1, one launch (start us, length us, event | category | flops | bytes accessed | tf_op | source)
XLA Modules:
  0.0 96.7 jit_solution(11492557117602487232)
XLA Ops:
  0.6 63.4 %gather.1 = (bf16[2,32,48,384]{3,2,1,0:T(8,128)(2,1)}, bf16[4,2,2,2,128,640]{5,4,3,2,1,0:T(8,128)(2,1)}, bf16[128,1536]{1,0:T(8,128)(2,1)}, f32[1,1536]{1,0:T(1,...) custom-call(bf16[48,1536]{1,0:T(8,128)(2,1)} %w_ref.1, ...), custom_call_target="tpu_custom_call" | custom-call | flops 2000000000 | bytes 20000000 | tf_op jit(solution)/shard_map/gather/pallas_call | solution.py:330
  64.0 16.8 %attend.1 = (bf16[2,4,128,512]{3,2,1,0:T(8,128)(2,1)}, f32[2,4,128,128]{3,2,1,0:T(8,128)}) custom-call(s32[32,32]{1,0:T(8,128)} %mask.1, bf16[2,1024,512]{2,1,0:T(8,128)(2,1)} %get-tuple-element.15.qg_ref, bf16[2,512,128]{2,1,0:T(8,128)(2,1)} %get-tuple-element.16.qr_ref, bf16[32,128,640]{2,1,0:T(8,128)(2,1)} %bitcast.5), custom_call_target="tpu_custom_call" | custom-call | flops 10000000000 | bytes 10000000 | tf_op jit(solution)/shard_map/attend/pallas_call | solution.py:499
  80.9 13.2 %reduce.1 = (f32[1,1536]{1,0:T(1,128)}, f32[1,1536]{1,0:T(1,128)}) custom-call(bf16[128,1536]{1,0:T(8,128)(2,1)} %q_ref.3, bf16[128,1536]{1,0:T(8,128)(2,1)} %get-tuple-element.11.xq_ref, f32[1,1536]{1,0:T(1,128)} %b_ref.3, f32[1,1536]{1,0:T(1,128)} %get-tuple-element.12.xb_ref, f32[1536]{0:T(1024)} %gain_ref.3, bf16[2,1536,384]{2,1,0:T(8,128)(2,1)} %bitcast.3, ...), custom_call_target="tpu_custom_call" | custom-call | tf_op jit(solution)/shard_map/reduce/pallas_call | solution.py:622
  94.1 1.3 %copy.15 = f32[1,1536]{1,0:T(1,128)} copy(f32[1,1536]{1,0:T(1,128)} %get-tuple-element.22) | data formatting | bytes 12288
  95.4 1.3 %copy.16 = f32[1,1536]{1,0:T(1,128)} copy(f32[1,1536]{1,0:T(1,128)} %get-tuple-element.23) | data formatting | bytes 12288

commit v4 on v3

--- a/solution.py
+++ b/solution.py
@@ -52,18 +52,16 @@
     core = lax.rem(k, 2)
     z_right = (a * NZ + lax.rem(z + 1, NZ), k)
     z_left = (a * NZ + lax.rem(z + NZ - 1, NZ), k)
-    first_hop = 2 - x_hi
-    z_first = tuple((a * NZ + lax.rem(z + NZ + way * first_hop, NZ), k) for way in (1, -1))
-    z_next = tuple((a * NZ + lax.rem(z + NZ + way * 2, NZ), k) for way in (1, -1))
+    z_right2 = (a * NZ + lax.rem(z + 2, NZ), k)
+    z_left2 = (a * NZ + lax.rem(z + NZ - 2, NZ), k)
     y_right = (c, x_hi * 8 + lax.rem(y + 1, NY) * 2 + core)
     y_left = (c, x_hi * 8 + lax.rem(y + NY - 1, NY) * 2 + core)
     sibling = (c, x_hi * 8 + y * 2 + (1 - core))
     pair = ((1 - a) * NZ + z, k)
     across = ((1 - a) * NZ + z, (1 - x_hi) * 8 + y * 2 + core)
-    far = (c, (1 - x_hi) * 8 + y * 2 + core)
 
     barrier = pltpu.get_barrier_semaphore()
-    for dev in (z_right, z_left, *z_first, *z_next, y_right, y_left, sibling, pair, across, far):
+    for dev in (z_right, z_left, z_right2, z_left2, y_right, y_left, sibling, pair, across):
         pl.semaphore_signal(barrier, inc=1, device_id=dev, device_id_type=MESH)
 
     my_d = pl.ds(pl.multiple_of(a * DCOLS, 128), DCOLS)
@@ -85,7 +83,7 @@
     load_k.wait()
     for copy in fills:
         copy.start()
-    pl.semaphore_wait(barrier, 12)
+    pl.semaphore_wait(barrier, 9)
 
     sends = []
 
@@ -130,78 +128,73 @@
 
     rows = pl.ds(pl.multiple_of(core * 64 + y * 16, 16), 16)
 
-    def z_slot(way, step):
-        at = jnp.where(x_hi == 0, 2 * step - 1, 2 * step - 2) + way
-        return KV.at[at // 2, a, x_hi, lax.rem(at, 2), rows]
+    def far(way, step):
+        return 0 if step == 0 else (2 * step if way else 2 * step - 1)
 
     def z_send(way, step):
-        src = own.at[rows] if step == 1 else z_slot(way, step - 1)
-        dev = (z_first if step == 1 else z_next)[way]
-        send(src, z_slot(way, step), z_s.at[way, step - 1], z_r.at[way, step - 1], dev)
+        hop = 1 if step == 1 else 2
+        src = own.at[rows] if step <= 2 else KV.at[a, far(way, step - 2), rows]
+        dev = (z_left if way else z_right) if hop == 1 else (z_left2 if way else z_right2)
+        send(src, KV.at[a, far(way, step), rows], z_s.at[way, step - 1], z_r.at[way, step - 1], dev)
 
     def kz(step):
-        def one(way):
-            got(z_slot(way, step), z_s.at[way, step - 1], z_r.at[way, step - 1])
-
-        one(0)
-        if step < 4:
-            z_send(0, step + 1)
-            one(1)
-            if step < 3:
-                z_send(1, step + 1)
-            else:
-                pl.when(x_hi == 1)(lambda: last_left().start())
-        else:
-            pl.when(x_hi == 1)(lambda: one(1))
-
-    def last_left():
-        return pltpu.make_async_remote_copy(
-            src_ref=KV.at[2, a, 1, 1, rows], dst_ref=KV.at[3, a, 1, 1, rows],
-            send_sem=z_s.at[1, 3], recv_sem=z_r.at[1, 3], device_id=z_next[1], device_id_type=MESH,
-        )
+        for way in range(2):
+            if step <= 8 - way:
+                got(KV.at[a, far(way, step), rows], z_s.at[way, step - 1], z_r.at[way, step - 1])
+                if step + 2 <= 8 - way:
+                    z_send(way, step + 2)
 
     def y_rows(shift):
         return pl.ds(pl.multiple_of(core * 64 + lax.rem(y + shift + NY, NY) * 16, 16), 16)
 
+    def block(far_side, first, count, row):
+        return KV.at[1 - a if far_side else a, pl.ds(first, count), row]
+
     def kx(q):
-        part = KV.at[q, a, x_hi, :, rows]
-        for n, dev in ((0, far), (1, across), (2, pair)):
+        for n, dev in ((0, pair), (1, across)):
+            part = block(0, 4 * q + 2 * n, 2, rows)
             send(part, part, x_s.at[n, q], x_r.at[n, q], dev)
 
-    def ky(q):
-        for n, side, parity in ((2, 1 - a, x_hi), (1, 1 - a, 1 - x_hi), (0, a, 1 - x_hi)):
-            got(KV.at[q, side, parity, :, rows], x_s.at[n, q], x_r.at[n, q])
-        part = KV.at[q, :, :, :, rows]
+    def ky(q, far_side):
+        if far_side:
+            for n in range(2):
+                got(block(1, 4 * q + 2 * n, 2, rows), x_s.at[n, q], x_r.at[n, q])
+        part = block(far_side, 4 * q, 4, rows)
         for way in range(2):
-            send(part, part, y_s.at[way, q], y_r.at[way, q], y_left if way else y_right)
-
-    def kf(q):
+            n = 2 * far_side + way
+            send(part, part, y_s.at[n, q], y_r.at[n, q], y_left if way else y_right)
+
+    def kf(q, far_side):
         for way in range(2):
+            n = 2 * far_side + way
             row = y_rows(1 if way else -1)
-            got(KV.at[q, :, :, :, row], y_s.at[way, q], y_r.at[way, q])
-            part = KV.at[q, way, :, :, row]
-            send(part, part, f_s.at[way, q], f_r.at[way, q], y_left if way else y_right)
+            got(block(far_side, 4 * q, 4, row), y_s.at[n, q], y_r.at[n, q])
+            part = block(far_side, 4 * q + 2 * way, 2, row)
+            send(part, part, f_s.at[n, q], f_r.at[n, q], y_left if way else y_right)
 
     half = pl.ds(pl.multiple_of(core * 64, 16), 64)
 
     def kc(q):
-        for way in range(2):
-            got(KV.at[q, way, :, :, y_rows(2)], f_s.at[way, q], f_r.at[way, q])
-        part = KV.at[q, :, :, :, half]
+        for far_side in range(2):
+            for way in range(2):
+                n = 2 * far_side + way
+                got(block(far_side, 4 * q + 2 * way, 2, y_rows(2)), f_s.at[n, q], f_r.at[n, q])
+        part = KV.at[:, pl.ds(4 * q, 4), half]
         send(part, part, c_s.at[q], c_r.at[q], sibling)
 
     for two in range(2):
         send(w_ref.at[:, columns(1 - a, two)], W.at[two, c], m_s.at[6 * two], m_r.at[6 * two], pair)
-    z_send(0, 1)
-    z_send(1, 1)
+    for step in (1, 2):
+        z_send(0, step)
+        z_send(1, step)
     for two in range(2):
         w_send(0, 0, two, 1)
         w_send(1, 0, two, 1)
     copy_w = [pltpu.make_async_copy(w_ref.at[:, columns(a, two)], W.at[two, c], loc.at[4 * two]) for two in range(2)]
     for copy in copy_w:
         copy.start()
-    copy_k = pltpu.make_async_copy(own.at[rows], KV.at[0, a, 0, 0, rows], loc.at[1])
-    pl.when(x_hi == 0)(lambda: copy_k.start())
+    copy_k = pltpu.make_async_copy(own.at[rows], KV.at[a, 0, rows], loc.at[1])
+    copy_k.start()
     q_rows = pl.ds(pl.multiple_of(core * 64, 16), 64)
     send(q_ref.at[q_rows], q2.at[1, q_rows], m_s.at[1], m_r.at[1], pair)
     send(d_ref.at[:, their_d], dv.at[1], m_s.at[3], m_r.at[3], pair)
@@ -233,34 +226,47 @@
         drains[-1].start()
 
     def kend(q):
-        got(KV.at[q, :, :, :, other], c_s.at[q], c_r.at[q])
-        store(KV.at[q], KV_out.at[q])
+        got(KV.at[:, pl.ds(4 * q, 4), other], c_s.at[q], c_r.at[q])
+        store(KV.at[:, pl.ds(4 * q, 4)], KV_out.at[:, pl.ds(4 * q, 4)])
 
     for copy in fills:
         copy.wait()
     norm(0)
     kz(1)
-    pl.when(x_hi == 0)(lambda: copy_k.wait())
+    kz(2)
+    copy_k.wait()
     kx(0)
+    ky(0, 0)
     w(1)
-    absorb_g(0)
-    kz(2)
+    kz(3)
+    ky(0, 1)
+    kz(4)
     kx(1)
-    ky(0)
+    ky(1, 0)
     w(2)
-    kz(3)
+    kf(0, 0)
+    kz(5)
+    ky(1, 1)
+    kz(6)
     kx(2)
-    kf(0)
-    ky(1)
+    ky(2, 0)
+    w(3)
+    kf(0, 1)
+    kf(1, 0)
     got(q2.at[1, q_rows], m_s.at[1], m_r.at[1])
     send(q2.at[1, q_rows], q2.at[1, q_rows], m_s.at[2], m_r.at[2], sibling)
-    w(3)
-    kz(4)
+    kz(7)
+    ky(2, 1)
+    kz(8)
     kx(3)
-    kf(1)
-    ky(2)
+    ky(3, 0)
+    w(4)
+    absorb_g(0)
+    kf(1, 1)
+    ky(3, 1)
+    w(5)
+    kf(2, 0)
     kc(0)
-    w(4)
     got(q2.at[1, other], m_s.at[2], m_r.at[2])
     got(dv.at[1], m_s.at[3], m_r.at[3])
     got(bv.at[1], m_s.at[4], m_r.at[4])
@@ -268,22 +274,19 @@
     store(q2.at[1], xq_out)
     store(bv.at[1], xb_out)
     norm(1)
-    ky(3)
-    kf(2)
+    w(6)
+    kf(2, 1)
+    kf(3, 0)
     kc(1)
-    w(5)
+    kend(0)
     absorb_g(1)
     store(qg.at[:, pl.ds(HALF * BLK, HALF * BLK)], qg_out.at[:, pl.ds(HALF * BLK, HALF * BLK)])
-    kend(0)
-    kf(3)
-    w(6)
+    w(7)
+    kf(3, 1)
     kc(2)
     kend(1)
-    w(7)
+    w(8)
     kc(3)
-    kend(2)
-    w(8)
-    kend(3)
     for copy in copy_w:
         copy.wait()
     store(W, W_out)
@@ -312,9 +315,10 @@
         done = pl.ds(2 * two * BLK, 2 * BLK)
         store(qg.at[:, done], qg_out.at[:, done])
     store(qr, qr_out)
+    kend(2)
+    kend(3)
     for copy in drains:
         copy.wait()
-    pl.when(x_hi == 1)(lambda: last_left().wait_send())
     for copy in sends:
         copy.wait_send()
 
@@ -326,7 +330,7 @@
     ql = q_latent.shape[1]
     rows = HALF * BLK
     w_shape = (2, 2 * NZ, w_q.shape[0], QTWO)
-    k_shape = (NZ // 4, 2, 2, 2, BLK, WIDE)
+    k_shape = (2, NZ, BLK, WIDE)
     return pl.pallas_call(
         gather_kernel,
         out_shape=(
@@ -355,8 +359,8 @@
             pltpu.VMEM((KVL, DCOLS), BF16),
             pltpu.VMEM((KVL, DCOLS), BF16),
             pltpu.VMEM((2, BLK, ql), BF16),
-            dma(8, 8), dma(8, 8), dma(2, 4), dma(2, 4), dma(2, 4), dma(2, 4), dma(2, 4), dma(2, 4),
-            dma(3, 4), dma(3, 4), dma(4), dma(4), dma(7), dma(7), dma(5), dma(6), dma(16),
+            dma(8, 8), dma(8, 8), dma(2, 8), dma(2, 8), dma(4, 4), dma(4, 4), dma(4, 4), dma(4, 4),
+            dma(2, 4), dma(2, 4), dma(4), dma(4), dma(7), dma(7), dma(5), dma(6), dma(16),
         ],
         compiler_params=pltpu.CompilerParams(
             collective_id=0, has_side_effects=True, vmem_limit_bytes=54 * 2**20
@@ -391,11 +395,9 @@
         block = c if i == 0 else lax.rem(c + NZ, 2 * NZ)
 
         def visit(j, n):
-            away = lax.rem(z - lax.rem(j, NZ) + NZ, NZ)
-            left = away > NZ // 2
-            hops = jnp.where(left, NZ - away, away)
-            slot = jnp.where(away == 0, 0, jnp.where(left, hops, hops - 1))
-            index[i, n] = ((slot // 2 * 2 + j // NZ) * 2 + lax.rem(hops, 2)) * 2 + lax.rem(slot, 2)
+            far = lax.rem(z - lax.rem(j, NZ) + NZ, NZ)
+            slot = jnp.where(far == 0, 0, jnp.where(far <= NZ // 2, 2 * far - 1, 2 * (NZ - far)))
+            index[i, n] = (j // NZ) * NZ + slot
             return n + jnp.where(mask[block, j] > 0, 1, 0)
 
         n = lax.fori_loop(0, 2 * NZ, visit, 0)

time: 97.3 us -> 87.2 us (0.90)
  the two profiles are of different devices: /device:TPU:1 before, /device:TPU:225 now
where the time goes in v4:
time: 87.2 us; the launch traced here: 86.6 us
  Pallas kernels  83.4 us (96%)
  local copies, waits for them, and re-layouts  2.57 us (3%)
    pallas_call x1, Pallas kernels, gather(): pl.pallas_call(gather_kernel, out_shape=(jax.ShapeDtypeStruct(w_shape, BF...  50 us
    pallas_call x1, Pallas kernels, attend(): pl.pallas_call(attend_kernel, out_shape=(jax.ShapeDtypeStruct((2, HALF, B...  20.7 us
    pallas_call x1, Pallas kernels, reduce(): pl.pallas_call(reduce_kernel, out_shape=(jax.ShapeDtypeStruct((1, 2 * QCO...  12.6 us
    unnamed x2, local copies, waits for them, and re-layouts  2.57 us

profile of v4, /device:TPU:225, one launch (start us, length us, event | category | flops | bytes accessed | tf_op | source)
XLA Modules:
  0.0 86.6 jit_solution(38821964506597962)
XLA Ops:
  0.6 50.0 %gather.1 = (bf16[2,32,48,384]{3,2,1,0:T(8,128)(2,1)}, bf16[2,16,128,640]{3,2,1,0:T(8,128)(2,1)}, bf16[128,1536]{1,0:T(8,128)(2,1)}, f32[1,1536]{1,0:T(1,128)}, ...) custom-call(bf16[48,1536]{1,0:T(8,128)(2,1)} %w_ref.1, ...), custom_call_target="tpu_custom_call" | custom-call | flops 2000000000 | bytes 20000000 | tf_op jit(solution)/shard_map/gather/pallas_call | solution.py:334
  50.6 20.7 %attend.1 = (bf16[2,4,128,512]{3,2,1,0:T(8,128)(2,1)}, f32[2,4,128,128]{3,2,1,0:T(8,128)}) custom-call(s32[32,32]{1,0:T(8,128)} %mask.1, bf16[2,1024,512]{2,1,0:T(8,128)(2,1)} %get-tuple-element.15.qg_ref, bf16[2,512,128]{2,1,0:T(8,128)(2,1)} %get-tuple-element.16.qr_ref, bf16[32,128,640]{2,1,0:T(8,128)(2,1)} %bitcast.5), custom_call_target="tpu_custom_call" | custom-call | flops 10000000000 | bytes 10000000 | tf_op jit(solution)/shard_map/attend/pallas_call | solution.py:501
  71.4 12.6 %reduce.1 = (f32[1,1536]{1,0:T(1,128)}, f32[1,1536]{1,0:T(1,128)}) custom-call(bf16[128,1536]{1,0:T(8,128)(2,1)} %q_ref.3, bf16[128,1536]{1,0:T(8,128)(2,1)} %get-tuple-element.11.xq_ref, f32[1,1536]{1,0:T(1,128)} %b_ref.3, f32[1,1536]{1,0:T(1,128)} %get-tuple-element.12.xb_ref, f32[1536]{0:T(1024)} %gain_ref.3, bf16[2,1536,384]{2,1,0:T(8,128)(2,1)} %bitcast.3, ...), custom_call_target="tpu_custom_call" | custom-call | tf_op jit(solution)/shard_map/reduce/pallas_call | solution.py:624
  84.0 1.3 %copy.15 = f32[1,1536]{1,0:T(1,128)} copy(f32[1,1536]{1,0:T(1,128)} %get-tuple-element.22) | data formatting | bytes 12288
  85.3 1.3 %copy.16 = f32[1,1536]{1,0:T(1,128)} copy(f32[1,1536]{1,0:T(1,128)} %get-tuple-element.23) | data formatting | bytes 12288

commit v5 on v4

--- a/solution.py
+++ b/solution.py
@@ -427,17 +427,6 @@
         def _():
             step(count - 1, 1)
 
-    def in_pairs(count, step):
-        def pair(t, _):
-            step(2 * t, 2)
-            return 0
-
-        lax.fori_loop(0, count // 2, pair, 0)
-
-        @pl.when(lax.rem(count, 2) == 1)
-        def _():
-            step(count - 1, 1)
-
     for i in range(2):
         n = live[i]
         count = chunks_of(n)
@@ -463,7 +452,7 @@
                     top = jnp.maximum(top, s[:, part * 128 : (part + 1) * 128])
             peak[...] = top
 
-        in_pairs(count, scores)
+        in_fours(count, scores)
         top = jnp.max(peak[...], axis=1, keepdims=True) * scale2
 
         def weigh(first, many):
@@ -478,7 +467,7 @@
             lsum[...] = low
             gsum[...] = gow
 
-        in_pairs(count, weigh)
+        in_fours(count, weigh)
         total = jnp.sum(lsum[...], axis=1, keepdims=True)
         ratio = jnp.sum(gsum[...], axis=1, keepdims=True) / total
 

time: 87.2 us -> 87.4 us (level)
  the two profiles are of different devices: /device:TPU:225 before, /device:TPU:1 now
where the time goes in v5:
time: 87.4 us; the launch traced here: 88.5 us
  Pallas kernels  85.3 us (98%)
  local copies, waits for them, and re-layouts  2.57 us (3%)
    pallas_call x1, Pallas kernels, gather(): pl.pallas_call(gather_kernel, out_shape=(jax.ShapeDtypeStruct(w_shape, BF...  57.2 us
    pallas_call x1, Pallas kernels, attend(): pl.pallas_call(attend_kernel, out_shape=(jax.ShapeDtypeStruct((2, HALF, B...  15.8 us
    pallas_call x1, Pallas kernels, reduce(): pl.pallas_call(reduce_kernel, out_shape=(jax.ShapeDtypeStruct((1, 2 * QCO...  12.3 us
    unnamed x2, local copies, waits for them, and re-layouts  2.57 us

profile of v5, /device:TPU:1, one launch (start us, length us, event | category | flops | bytes accessed | tf_op | source)
XLA Modules:
  0.0 88.5 jit_solution(15903626233841400884)
XLA Ops:
  0.6 57.2 %gather.1 = (bf16[2,32,48,384]{3,2,1,0:T(8,128)(2,1)}, bf16[2,16,128,640]{3,2,1,0:T(8,128)(2,1)}, bf16[128,1536]{1,0:T(8,128)(2,1)}, f32[1,1536]{1,0:T(1,128)}, ...) custom-call(bf16[48,1536]{1,0:T(8,128)(2,1)} %w_ref.1, ...), custom_call_target="tpu_custom_call" | custom-call | flops 2000000000 | bytes 20000000 | tf_op jit(solution)/shard_map/gather/pallas_call | solution.py:334
  57.9 15.8 %attend.1 = (bf16[2,4,128,512]{3,2,1,0:T(8,128)(2,1)}, f32[2,4,128,128]{3,2,1,0:T(8,128)}) custom-call(s32[32,32]{1,0:T(8,128)} %mask.1, bf16[2,1024,512]{2,1,0:T(8,128)(2,1)} %get-tuple-element.15.qg_ref, bf16[2,512,128]{2,1,0:T(8,128)(2,1)} %get-tuple-element.16.qr_ref, bf16[32,128,640]{2,1,0:T(8,128)(2,1)} %bitcast.5), custom_call_target="tpu_custom_call" | custom-call | flops 10000000000 | bytes 10000000 | tf_op jit(solution)/shard_map/attend/pallas_call | solution.py:490
  73.7 12.3 %reduce.1 = (f32[1,1536]{1,0:T(1,128)}, f32[1,1536]{1,0:T(1,128)}) custom-call(bf16[128,1536]{1,0:T(8,128)(2,1)} %q_ref.3, bf16[128,1536]{1,0:T(8,128)(2,1)} %get-tuple-element.11.xq_ref, f32[1,1536]{1,0:T(1,128)} %b_ref.3, f32[1,1536]{1,0:T(1,128)} %get-tuple-element.12.xb_ref, f32[1536]{0:T(1024)} %gain_ref.3, bf16[2,1536,384]{2,1,0:T(8,128)(2,1)} %bitcast.3, ...), custom_call_target="tpu_custom_call" | custom-call | tf_op jit(solution)/shard_map/reduce/pallas_call | solution.py:613
  86.0 1.3 %copy.15 = f32[1,1536]{1,0:T(1,128)} copy(f32[1,1536]{1,0:T(1,128)} %get-tuple-element.22) | data formatting | bytes 12288
  87.3 1.3 %copy.16 = f32[1,1536]{1,0:T(1,128)} copy(f32[1,1536]{1,0:T(1,128)} %get-tuple-element.23) | data formatting | bytes 12288
